TPU v7x, 32 devices: a whole 2x2x4 slice. The times are simulated.
32 devices in a mesh: shard: 2 (over core), seq: 4 (over y, x), replica: 4 (over z).
Axes of the slice: x: 2, y: 2, z: 4, core: 2. Of those that a mesh axis runs over, the one named last changes fastest.
Arguments:
- tokens: bfloat16 [16, 256, 2048], P(('shard', 'replica'), 'seq'), may hold values from -6 to 6
- cotangent: bfloat16 [16, 256, 2048], P(('shard', 'replica'), 'seq'), may hold values from -6 to 6
- lengths: int32 [16], P(('shard', 'replica')), may hold values from 64 to 256, as said below
- norm_gains: bfloat16 [2, 2048], P(None, 'shard'), may hold values from 0.5 to 1.5
- w_in: bfloat16 [2048, 12288], P('shard'), may hold values from -0.125 to 0.125
- w_ab: bfloat16 [2048, 32], P('shard'), may hold values from -0.125 to 0.125
- conv_weight: bfloat16 [4, 8192], P(None, 'shard'), may hold values from -3 to 3
- gate_params: float32 [2, 16], replicated, as said below
- onorm_gain: float32 [256], replicated, may hold values from 0.5 to 1.5
- w_o: bfloat16 [4096, 2048], P('shard'), may hold values from -0.09375 to 0.09375
- w_gu: bfloat16 [2048, 11264], P('shard'), may hold values from -0.125 to 0.125
- w_down: bfloat16 [5632, 2048], P('shard'), may hold values from -0.078125 to 0.078125
Outputs:
- output: bfloat16 [16, 256, 2048], P(('shard', 'replica'), 'seq')
- input_grad: bfloat16 [16, 256, 2048], P(('shard', 'replica'), 'seq')
- norm_gains_grad: float32 [2, 2048], P(None, ('shard', 'seq'))
- w_in_grad: float32 [2048, 12288], P(('shard', 'seq'))
- w_ab_grad: float32 [2048, 32], P(('shard', 'seq'))
- conv_grad: float32 [4, 8192], P(None, ('shard', 'seq'))
- gate_params_grad: float32 [2, 16], replicated
- onorm_grad: float32 [256], replicated
- w_o_grad: float32 [4096, 2048], P(('shard', 'seq'))
- w_gu_grad: float32 [2048, 11264], P(('shard', 'seq'))
- w_down_grad: float32 [5632, 2048], P(('shard', 'seq'))
Inputs may be any that keep to these rules, and one draw needn't show every extreme that they name: `lengths`: each aligned run of 2 slots holds one slot of exactly 256 valid tokens; positions from a slot's length on are padding. `gate_params`: row 0 holds the logarithms of the heads' decay speeds, row 1 the biases added before the softplus.
All inputs are finite; a program needn't handle non-finite values.
Results may differ from a plain program's by a relative error of at most 0.017.
Values may be sent and summed in bfloat16 or wider, within the bound.
No kernel may reach another device: no remote copies, remote signals or barrier semaphores. Data moves between devices by JAX's collectives and lax.ppermute only.
A program may use at most 576 MiB of HBM per device.

v0:
```python
import functools

import jax
import jax.numpy as jnp
from jax import lax
from jax.experimental import pallas as pl
from jax.experimental.pallas import tpu as pltpu
from jax.sharding import PartitionSpec as P

D = 2048
HEADS = 16
DK = 128
DV = 256
FF = 5632
KERNEL = 4
KD = 2048
VD = 4096
CONVW = 8192
PROJW = 12288
EPS = 1e-06
HIGHEST = lax.Precision.HIGHEST
LOWEST_DECAY = -104.0
F32 = jnp.float32
BF16 = jnp.bfloat16
EVERY = ("shard", "seq", "replica")
GROUP = ("shard", "seq")


def mm(left, right, dims=((1,), (0,))):
    return lax.dot_general(
        left.astype(BF16), right.astype(BF16), (dims, ((), ())), preferred_element_type=F32
    )


def split(value):
    high = value.astype(BF16)
    return high, (value - high.astype(F32)).astype(BF16)


def mm3s(left, right, dims=((1,), (0,))):
    return (
        mm(left[0], right[0], dims) + mm(left[0], right[1], dims) + mm(left[1], right[0], dims)
    )


def mm3(left, right, dims=((1,), (0,))):
    return mm3s(split(left), split(right), dims)


ROWS_ROWS = ((1,), (1,))
COLS_COLS = ((0,), (0,))


def delayed(value, steps, rows):
    if steps == 0:
        return value
    return jnp.where(rows >= steps, pltpu.roll(value, steps, 0), 0.0)


def advanced(value, steps, rows):
    if steps == 0:
        return value
    length = value.shape[0]
    return jnp.where(rows < length - steps, pltpu.roll(value, length - steps, 0), 0.0)


def convolved(source, taps, rows):
    mixed = taps[KERNEL - 1 : KERNEL] * source
    for offset in range(KERNEL - 1):
        mixed = mixed + taps[offset : offset + 1] * delayed(source, KERNEL - 1 - offset, rows)
    return mixed


def unit(value):
    scale = lax.rsqrt(jnp.sum(value * value, -1, keepdims=True) + EPS)
    return value * scale, scale


def decay_matrices(rates):
    length = rates.shape[1]
    row_ids = lax.broadcasted_iota(jnp.int32, (length, length), 0)
    col_ids = lax.broadcasted_iota(jnp.int32, (length, length), 1)
    decay_row = rates[0:1]
    rate_row = rates[1:2]
    diagonal = row_ids == col_ids
    running = jnp.sum(jnp.where(row_ids >= col_ids, decay_row, 0.0), 1, keepdims=True)
    running_row = jnp.sum(jnp.where(diagonal, running, 0.0), 0, keepdims=True)
    rate = jnp.sum(jnp.where(diagonal, rate_row, 0.0), 1, keepdims=True)
    spread = jnp.minimum(running - running_row, 0.0)
    weight = jnp.where(row_ids >= col_ids, jnp.exp(spread), 0.0)
    return row_ids, col_ids, rate, weight


def lower_inverses(systems, row_ids, col_ids):
    length = row_ids.shape[0]
    eye = (row_ids == col_ids).astype(F32)
    same = jnp.bitwise_xor(row_ids, col_ids)
    inverses = [eye - jnp.where(same < 2, system, 0.0) for system in systems]
    size = 2
    while size < length:
        level = (same >= size) & (same < 2 * size)
        halves = [split(inverse) for inverse in inverses]
        inner = [
            mm3s(split(jnp.where(level, system, 0.0)), half)
            for system, half in zip(systems, halves)
        ]
        inverses = [
            inverse - mm3s(half, split(item))
            for inverse, half, item in zip(inverses, halves, inner)
        ]
        size *= 2
    return inverses


def head_inputs(source, taps):
    rows = lax.broadcasted_iota(jnp.int32, (source.shape[0], 1), 0)
    cuts = (0, DK, 2 * DK, 2 * DK + DV)
    raw = [source[:, low:high].astype(BF16).astype(F32) for low, high in zip(cuts, cuts[1:])]
    mixed = [convolved(item, kernel, rows) for item, kernel in zip(raw, taps)]
    slopes = [jax.nn.sigmoid(item) for item in mixed]
    query_unit, query_scale = unit(mixed[0] * slopes[0])
    key_rows, key_scale = unit(mixed[1] * slopes[1])
    values = mixed[2] * slopes[2]
    queries = query_unit * DK ** (-0.5)
    return raw, rows, mixed, slopes, queries, key_rows, values, query_unit, query_scale, key_scale


def slot_rows(ref, place, slot, low, high):
    pieces = ref.shape[0]
    return jnp.concatenate(
        [ref[jnp.bitwise_xor(place, j), slot, :, low:high] for j in range(pieces)], 0
    )


def taps_of(refs, head):
    return [
        ref[:, head * width : (head + 1) * width].astype(F32)
        for ref, width in zip(refs, (DK, DK, DV))
    ]


def forward_kernel(
    place_ref, proj_ref, taps_q, taps_k, taps_v, rates_ref, gain_ref, *outs
):
    *gated_refs, inverse_ref, update_ref, kept = outs
    place = place_ref[0]
    micro, together = rates_ref.shape[0], rates_ref.shape[1]
    pairs = [(slot, head) for slot in range(micro) for head in range(together)]
    work = []
    for slot, head in pairs:
        source = slot_rows(proj_ref, place, slot, head * HEAD_WIDTH, (head + 1) * HEAD_WIDTH)
        items = head_inputs(source, taps_of((taps_q, taps_k, taps_v), head))
        queries, key_rows, values = items[4:7]
        row_ids, col_ids, rate, weight = decay_matrices(rates_ref[slot, head])
        system = jnp.where(
            row_ids > col_ids, rate * mm3(key_rows, key_rows, ROWS_ROWS) * weight, 0.0
        )
        scores = (mm(queries, key_rows, ROWS_ROWS) * weight).astype(BF16)
        gate = source[:, 2 * DK + DV :]
        work.append((system, scores, rate * values, gate * jax.nn.sigmoid(gate)))
    inverses = lower_inverses([item[0] for item in work], row_ids, col_ids)
    row = proj_ref.shape[2]
    for (slot, head), item, inverse in zip(pairs, work, inverses):
        update = mm3(inverse, item[2])
        outputs = mm(item[1], update)
        scaled = (
            outputs
            * lax.rsqrt(jnp.mean(outputs * outputs, -1, keepdims=True) + EPS)
            * gain_ref[...]
        )
        inverse_ref[slot, head] = inverse
        update_ref[slot, head] = update
        kept[...] = (scaled * item[3]).reshape(kept.shape)
        for step, ref in enumerate(gated_refs):
            ref[slot, :, head * DV : (head + 1) * DV] = kept[jnp.bitwise_xor(place, step)].astype(
                ref.dtype
            )


def unit_back(grad, direction, scale):
    return scale * (grad - direction * jnp.sum(grad * direction, -1, keepdims=True))


def backward_kernel(
    place_ref, proj_ref, taps_q, taps_k, taps_v, rates_ref, gain_ref, inverse_ref, update_ref,
    *refs,
):
    *grad_refs, dproj_ref, small_ref, taken, kept = refs
    place = place_ref[0]
    micro, together = rates_ref.shape[0], rates_ref.shape[1]
    small_ref[...] = jnp.zeros_like(small_ref)
    for slot in range(micro):
        for head in range(together):
            backward_head(
                place, slot, head, proj_ref, (taps_q, taps_k, taps_v), rates_ref, gain_ref,
                inverse_ref, update_ref, grad_refs, dproj_ref, small_ref,
                taken.at[slot, head], kept.at[slot, head],
            )


def backward_head(
    place, slot, head, proj_ref, taps_refs, rates_ref, gain_ref, inverse_ref, update_ref,
    grad_refs, dproj_ref, small_ref, taken, kept,
):
    source = slot_rows(proj_ref, place, slot, head * HEAD_WIDTH, (head + 1) * HEAD_WIDTH)
    taps = taps_of(taps_refs, head)
    raw, rows, mixed, slopes, queries, key_rows, values, query_unit, query_scale, key_scale = (
        head_inputs(source, taps)
    )
    for step, ref in enumerate(grad_refs):
        taken[jnp.bitwise_xor(place, step)] = ref[slot, :, head * DV : (head + 1) * DV]
    upstream = jnp.concatenate([taken[j] for j in range(len(grad_refs))], 0).astype(F32)
    row_ids, col_ids, rate, weight = decay_matrices(rates_ref[slot, head])
    inner = mm3(key_rows, key_rows, ROWS_ROWS)
    strict = row_ids > col_ids
    keyed = jnp.where(strict, inner * weight, 0.0)
    scores = mm(queries, key_rows, ROWS_ROWS) * weight
    inverse = inverse_ref[slot, head]
    update = update_ref[slot, head]
    outputs = mm(scores, update)
    gate = source[:, 2 * DK + DV :]
    gate_slope = jax.nn.sigmoid(gate)
    out_scale = lax.rsqrt(jnp.mean(outputs * outputs, -1, keepdims=True) + EPS)
    out_unit = outputs * out_scale
    gain = gain_ref[...]
    scaled_grad = upstream * (gate * gate_slope)
    gate_grad = upstream * out_unit * gain * (gate_slope * (1.0 + gate * (1.0 - gate_slope)))
    gain_grad = jnp.sum(scaled_grad * out_unit, 0, keepdims=True)
    unit_grad = scaled_grad * gain
    out_grad = out_scale * (
        unit_grad - out_unit * jnp.mean(unit_grad * out_unit, -1, keepdims=True)
    )
    scores_grad = jnp.where(row_ids >= col_ids, mm(out_grad, update, ROWS_ROWS), 0.0)
    update_grad = mm(scores, out_grad, COLS_COLS)
    target_grad = mm3(inverse, update_grad, COLS_COLS)
    system_grad = jnp.where(strict, -mm(target_grad, update, ROWS_ROWS), 0.0)
    value_grad = rate * target_grad
    keyed_grad = system_grad * keyed
    rate_grad = jnp.sum(target_grad * values, 1, keepdims=True) + jnp.sum(
        keyed_grad, 1, keepdims=True
    )
    spread_grad = keyed_grad * rate + scores_grad * scores
    inner_grad = system_grad * weight * rate
    raw_scores_grad = scores_grad * weight
    query_grad = mm(raw_scores_grad, key_rows) * DK ** (-0.5)
    key_grad = (
        mm(raw_scores_grad, queries, COLS_COLS)
        + mm(inner_grad, key_rows)
        + mm(inner_grad, key_rows, COLS_COLS)
    )
    diagonal = row_ids == col_ids
    column_sum = jnp.sum(spread_grad, 0, keepdims=True)
    running_grad = jnp.sum(spread_grad, 1, keepdims=True) - jnp.sum(
        jnp.where(diagonal, column_sum, 0.0), 1, keepdims=True
    )
    decay_grad = jnp.sum(jnp.where(row_ids >= col_ids, running_grad, 0.0), 0, keepdims=True)
    rate_grad_row = jnp.sum(jnp.where(diagonal, rate_grad, 0.0), 0, keepdims=True)
    active_grads = (
        unit_back(query_grad, query_unit, query_scale),
        unit_back(key_grad, key_rows, key_scale),
        value_grad,
    )
    cuts = (0, DK, 2 * DK, 2 * DK + DV, HEAD_WIDTH)
    for low, high, grad_out, plain, before, slope, kernel in zip(
        cuts, cuts[1:], active_grads, raw, mixed, slopes, taps
    ):
        mixed_grad = grad_out * (slope * (1.0 + before * (1.0 - slope)))
        total = kernel[KERNEL - 1 : KERNEL] * mixed_grad
        for offset in range(KERNEL):
            steps = KERNEL - 1 - offset
            if steps:
                total = total + kernel[offset : offset + 1] * advanced(mixed_grad, steps, rows)
            small_ref[slot, head, offset : offset + 1, low:high] = jnp.sum(
                mixed_grad * delayed(plain, steps, rows), 0, keepdims=True
            )
        kept[:, :, low:high] = total.reshape(kept.shape[:2] + (high - low,))
    kept[:, :, cuts[3] : cuts[4]] = gate_grad.reshape(kept.shape[:2] + (DV,))
    for step in range(kept.shape[0]):
        dproj_ref[step, slot, :, head * HEAD_WIDTH : (head + 1) * HEAD_WIDTH] = kept[
            jnp.bitwise_xor(place, step)
        ].astype(dproj_ref.dtype)
    small_ref[slot, head, 4:5, 0:DV] = gain_grad
    length = decay_grad.shape[1]
    small_ref[slot, head, 5:6, 0:length] = decay_grad
    small_ref[slot, head, 6:7, 0:length] = rate_grad_row


VMEM_LIMIT = 56 * 1024 * 1024
HEAD_WIDTH = 2 * DK + 2 * DV
SMALL_ROWS = 8


def mixer_specs(pieces, micro, row, heads, length, together):
    def slots(width):
        return pl.BlockSpec((micro, row, together * width), lambda h, place: (0, 0, h))

    def taps(width, first):
        at = first // (together * width)
        return pl.BlockSpec(
            (KERNEL, together * width),
            lambda h, place: (0, at + place[0] * (heads // together) + h),
        )

    proj = pl.BlockSpec(
        (pieces, micro, row, together * HEAD_WIDTH), lambda h, place: (0, 0, 0, h)
    )
    kernel = [taps(DK, 0), taps(DK, KD), taps(DV, 2 * KD)]
    rates = pl.BlockSpec((micro, together, SMALL_ROWS, length), lambda h, place: (0, h, 0, 0))
    gain = pl.BlockSpec((1, DV), lambda h, place: (0, 0))

    def square(width):
        return pl.BlockSpec((micro, together, length, width), lambda h, place: (0, h, 0, 0))

    return slots, proj, kernel, rates, gain, square


def mixer_forward(place, projected, taps, rates, gain, together):
    pieces, micro, row, _ = projected.shape
    heads, length = rates.shape[1], rates.shape[3]
    slots, proj, kernel, rate_spec, gain_spec, square = mixer_specs(
        pieces, micro, row, heads, length, together
    )
    return pl.pallas_call(
        forward_kernel,
        grid_spec=pltpu.PrefetchScalarGridSpec(
            num_scalar_prefetch=1,
            grid=(heads // together,),
            in_specs=[proj] + kernel + [rate_spec, gain_spec],
            out_specs=[slots(DV)] * pieces + [square(length), square(DV)],
            scratch_shapes=[pltpu.VMEM((pieces, row, DV), F32)],
        ),
        out_shape=[jax.ShapeDtypeStruct((micro, row, heads * DV), BF16)] * pieces
        + [
            jax.ShapeDtypeStruct((micro, heads, length, length), F32),
            jax.ShapeDtypeStruct((micro, heads, length, DV), F32),
        ],
        compiler_params=pltpu.CompilerParams(vmem_limit_bytes=VMEM_LIMIT),
        name="mixer_forward",
    )(place, projected, taps, taps, taps, rates, gain)


def mixer_backward(place, projected, taps, rates, gain, inverse, update, grads, together):
    pieces, micro, row, _ = projected.shape
    heads, length = rates.shape[1], rates.shape[3]
    slots, proj, kernel, rate_spec, gain_spec, square = mixer_specs(
        pieces, micro, row, heads, length, together
    )
    small_width = 2 * DK + DV
    return pl.pallas_call(
        backward_kernel,
        grid_spec=pltpu.PrefetchScalarGridSpec(
            num_scalar_prefetch=1,
            grid=(heads // together,),
            in_specs=[proj]
            + kernel
            + [rate_spec, gain_spec, square(length), square(DV)]
            + [slots(DV)] * pieces,
            out_specs=[
                proj,
                pl.BlockSpec(
                    (micro, together, SMALL_ROWS, small_width), lambda h, place: (0, h, 0, 0)
                ),
            ],
            scratch_shapes=[
                pltpu.VMEM((micro, together, pieces, row, DV), BF16),
                pltpu.VMEM((micro, together, pieces, row, HEAD_WIDTH), F32),
            ],
        ),
        out_shape=[
            jax.ShapeDtypeStruct((pieces, micro, row, heads * HEAD_WIDTH), BF16),
            jax.ShapeDtypeStruct((micro, heads, SMALL_ROWS, small_width), F32),
        ],
        compiler_params=pltpu.CompilerParams(vmem_limit_bytes=VMEM_LIMIT),
        name="mixer_backward",
    )(place, projected, taps, taps, taps, rates, gain, inverse, update, *grads)


def pick_kernel(place_ref, q_ref, k_ref, v_ref, g_ref, out_ref):
    at = 0
    for ref in (q_ref, k_ref, v_ref, g_ref):
        out_ref[:, at : at + ref.shape[1]] = ref[...]
        at += ref.shape[1]


def pick_heads(place, w_in, heads):
    depth = w_in.shape[0]

    def one(width, first):
        at = first // width
        return pl.BlockSpec((depth, width), lambda h, place: (0, at + place[0] * heads + h))

    return pl.pallas_call(
        pick_kernel,
        grid_spec=pltpu.PrefetchScalarGridSpec(
            num_scalar_prefetch=1,
            grid=(heads,),
            in_specs=[one(DK, 0), one(DK, KD), one(DV, 2 * KD), one(DV, CONVW)],
            out_specs=pl.BlockSpec((depth, HEAD_WIDTH), lambda h, place: (0, h)),
        ),
        out_shape=jax.ShapeDtypeStruct((depth, heads * HEAD_WIDTH), w_in.dtype),
        compiler_params=pltpu.CompilerParams(vmem_limit_bytes=VMEM_LIMIT),
        name="pick_heads",
    )(place, w_in, w_in, w_in, w_in)


def project_kernel(parts, pieces, place_ref, gain_ref, *refs):
    piece_refs, weight_refs = refs[:pieces], refs[pieces : pieces + parts]
    normed_ref, out_ref = refs[pieces + parts :]
    rows = piece_refs[0].shape[0]

    @pl.when(pl.program_id(0) == 0)
    def _():
        for at, ref in enumerate(piece_refs):
            values = ref[...].astype(F32)
            scale = lax.rsqrt(jnp.mean(values * values, -1, keepdims=True) + EPS)
            normed_ref[at * rows : (at + 1) * rows] = (values * scale * gain_ref[...]).astype(BF16)

    total = None
    for step, ref in enumerate(weight_refs):
        depth = ref.shape[0]
        at = pl.multiple_of(jnp.bitwise_xor(place_ref[0], step) * depth, 128)
        term = jnp.dot(normed_ref[:, pl.ds(at, depth)], ref[...], preferred_element_type=F32)
        total = term if total is None else total + term
    out_ref[...] = total


def project(shard_place, gain, piece_list, weights):
    rows, width = piece_list[0].shape
    columns = weights[0].shape[1]
    tile = HEAD_WIDTH
    pieces, parts = len(piece_list), len(weights)
    whole = pl.BlockSpec((rows, width), lambda j, place: (0, 0))
    return pl.pallas_call(
        functools.partial(project_kernel, parts, pieces),
        grid_spec=pltpu.PrefetchScalarGridSpec(
            num_scalar_prefetch=1,
            grid=(columns // tile,),
            in_specs=[pl.BlockSpec((1, width), lambda j, place: (0, 0))]
            + [whole] * pieces
            + [pl.BlockSpec((weights[0].shape[0], tile), lambda j, place: (0, j))] * parts,
            out_specs=[
                pl.BlockSpec((pieces * rows, width), lambda j, place: (0, 0)),
                pl.BlockSpec((pieces * rows, tile), lambda j, place: (0, j)),
            ],
        ),
        out_shape=[
            jax.ShapeDtypeStruct((pieces * rows, width), BF16),
            jax.ShapeDtypeStruct((pieces * rows, columns), F32),
        ],
        compiler_params=pltpu.CompilerParams(vmem_limit_bytes=VMEM_LIMIT),
        name="project",
    )(shard_place, gain, *piece_list, *weights)


def head_rows(places_ref, step, rows, group):
    width = min(rows, group)
    found = []
    for at in range(rows // width):
        first = jnp.bitwise_xor(places_ref[1], step) * rows + at * width
        whose = jnp.bitwise_xor(first // group, places_ref[0])
        found.append((whose, pl.multiple_of(first % group, 128) if width < group else 0, width))
    return found


def merge_kernel(parts, pieces, places_ref, gain_ref, tokens_ref, *refs):
    mixed_refs, weight_refs = refs[:pieces], refs[pieces : pieces + parts]
    middle_ref, normed_ref, *left_refs, gathered = refs[pieces + parts :]
    step_id = pl.program_id(0)
    group = mixed_refs[0].shape[1]

    @pl.when(step_id == 0)
    def _():
        for at, ref in enumerate(mixed_refs):
            gathered[at] = ref[...]
        height = left_refs[0].shape[1] // parts
        for at, ref in enumerate(left_refs):
            for part in range(parts):
                first = (part * pieces + jnp.bitwise_xor(places_ref[0], at)) * height
                whose = jnp.bitwise_xor(first // group, places_ref[0])
                ref[:, part * height : (part + 1) * height] = gathered[
                    whose, :, pl.ds(pl.multiple_of(first % group, 128), height)
                ]

    tile = weight_refs[0].shape[1]
    total = tokens_ref[...].astype(F32)
    for step, ref in enumerate(weight_refs):
        rows = ref.shape[0]
        for at, (whose, first, width) in enumerate(head_rows(places_ref, step, rows, group)):
            total = total + jnp.dot(
                gathered[whose, :, pl.ds(first, width)],
                ref[at * width : (at + 1) * width],
                preferred_element_type=F32,
            )
    middle_ref[:, pl.ds(pl.multiple_of(step_id * tile, 128), tile)] = total

    @pl.when(step_id == pl.num_programs(0) - 1)
    def _():
        values = middle_ref[...]
        scale = lax.rsqrt(jnp.mean(values * values, -1, keepdims=True) + EPS)
        normed_ref[...] = (values * scale * gain_ref[...]).astype(BF16)


def merge(places, gain, tokens, mixed, weights):
    rows, width = tokens.shape
    tile = 512
    pieces, parts = len(mixed), len(weights)
    group = mixed[0].shape[1]
    whole = pl.BlockSpec((rows, width), lambda j, place: (0, 0))
    return pl.pallas_call(
        functools.partial(merge_kernel, parts, pieces),
        grid_spec=pltpu.PrefetchScalarGridSpec(
            num_scalar_prefetch=1,
            grid=(width // tile,),
            in_specs=[
                pl.BlockSpec((1, width), lambda j, place: (0, 0)),
                pl.BlockSpec((rows, tile), lambda j, place: (0, j)),
            ]
            + [pl.BlockSpec((rows, group), lambda j, place: (0, 0))] * pieces
            + [pl.BlockSpec((weights[0].shape[0], tile), lambda j, place: (0, j))] * parts,
            out_specs=[whole, whole]
            + [pl.BlockSpec((rows, group), lambda j, place: (0, 0))] * pieces,
            scratch_shapes=[pltpu.VMEM((pieces, rows, group), BF16)],
        ),
        out_shape=[
            jax.ShapeDtypeStruct((rows, width), F32),
            jax.ShapeDtypeStruct((rows, width), BF16),
        ]
        + [jax.ShapeDtypeStruct((rows, group), BF16)] * pieces,
        compiler_params=pltpu.CompilerParams(vmem_limit_bytes=VMEM_LIMIT),
        name="merge_heads",
    )(places, gain, tokens, *mixed, *weights)


def feed_kernel(parts, places_ref, *refs):
    normed_refs, grad_ref = refs[:parts], refs[parts]
    gate_refs, wide_refs = refs[parts + 1 : 2 * parts + 1], refs[2 * parts + 1 : 3 * parts + 1]
    outs, hidden_ref = refs[3 * parts + 1 : 4 * parts + 1], refs[4 * parts + 1]
    normed_all, grad_all = refs[4 * parts + 2 :]
    step_id = pl.program_id(0)
    rows, depth = normed_refs[0].shape[0], gate_refs[0].shape[0]

    @pl.when(step_id == 0)
    def _():
        for at in range(parts):
            where = slice(at * rows, (at + 1) * rows)
            for step in range(parts):
                first = pl.multiple_of(jnp.bitwise_xor(places_ref[1], step) * depth, 128)
                normed_all[step, where] = normed_refs[at][:, pl.ds(first, depth)]
        grad_all[...] = jnp.zeros_like(grad_all)

    gate, wide = None, None
    for step in range(parts):
        left = normed_all[step]
        one = jnp.dot(left, gate_refs[step][...], preferred_element_type=F32)
        two = jnp.dot(left, wide_refs[step][...], preferred_element_type=F32)
        gate, wide = (one, two) if gate is None else (gate + one, wide + two)
    hidden_grad = grad_ref[...]
    slope = jax.nn.sigmoid(gate)
    hidden_ref[...] = (gate * slope * wide).astype(BF16)
    gate_grad = (hidden_grad * wide * (slope * (1.0 + gate * (1.0 - slope)))).astype(BF16)
    wide_grad = (hidden_grad * gate * slope).astype(BF16)
    for step in range(parts):
        grad_all[step] += mm(gate_grad, gate_refs[step][...], ROWS_ROWS) + mm(
            wide_grad, wide_refs[step][...], ROWS_ROWS
        )

    @pl.when(step_id == pl.num_programs(0) - 1)
    def _():
        for at in range(parts):
            where = slice(at * rows, (at + 1) * rows)
            for step in range(parts):
                outs[at][step ^ at] = grad_all[step, where]


def feed(places, normed, hidden_grad, weights):
    rows, width = normed[0].shape
    parts = len(weights)
    depth = weights[0].shape[0]
    shard_columns = hidden_grad.shape[1]
    tile = 256 if shard_columns % 256 == 0 else shard_columns
    if tile == 256:
        sources = [(part, part) for part in weights]
        columns = weights[0].shape[1] // 2
        gate_at = lambda j, place: (0, place[1] * (shard_columns // tile) + j)
        wide_at = lambda j, place: (
            0,
            columns // tile + place[1] * (shard_columns // tile) + j,
        )
    else:
        shard = lax.axis_index("shard")
        sources = [
            (
                part_of(part[:, : part.shape[1] // 2], shard, parts, 1),
                part_of(part[:, part.shape[1] // 2 :], shard, parts, 1),
            )
            for part in weights
        ]
        gate_at = wide_at = lambda j, place: (0, j)
    whole = pl.BlockSpec((rows, width), lambda j, place: (0, 0))
    narrow = pl.BlockSpec((parts * rows, tile), lambda j, place: (0, j))
    return pl.pallas_call(
        functools.partial(feed_kernel, parts),
        grid_spec=pltpu.PrefetchScalarGridSpec(
            num_scalar_prefetch=1,
            grid=(shard_columns // tile,),
            in_specs=[whole] * parts
            + [narrow]
            + [pl.BlockSpec((depth, tile), gate_at)] * parts
            + [pl.BlockSpec((depth, tile), wide_at)] * parts,
            out_specs=[pl.BlockSpec((parts, rows, depth), lambda j, place: (0, 0, 0))] * parts
            + [narrow],
            scratch_shapes=[
                pltpu.VMEM((parts, parts * rows, depth), BF16),
                pltpu.VMEM((parts, parts * rows, depth), F32),
            ],
        ),
        out_shape=[jax.ShapeDtypeStruct((parts, rows, depth), F32)] * parts
        + [jax.ShapeDtypeStruct((parts * rows, shard_columns), BF16)],
        compiler_params=pltpu.CompilerParams(vmem_limit_bytes=VMEM_LIMIT),
        name="feed_forward",
    )(
        places,
        *normed,
        hidden_grad,
        *[source[0] for source in sources],
        *[source[1] for source in sources],
    )


def unmerge_kernel(parts, pieces, places_ref, gain_ref, middle_ref, up_ref, *refs):
    grad_refs, weight_refs = refs[:parts], refs[parts : 2 * parts]
    grad_out, sent_out, gain_out = refs[2 * parts : 2 * parts + 3]
    piece_outs = refs[2 * parts + 3 : 2 * parts + 3 + pieces]
    gathered = refs[-1]
    step_id = pl.program_id(0)
    depth = grad_refs[0].shape[2]

    @pl.when(step_id == 0)
    def _():
        for step in range(parts):
            first = pl.multiple_of(jnp.bitwise_xor(places_ref[1], step) * depth, 128)
            total = grad_refs[0][step]
            for ref in grad_refs[1:]:
                total = total + ref[step]
            grad_out[:, pl.ds(first, depth)] = total
        values, grad, gain = middle_ref[...], grad_out[...], gain_ref[...]
        scale = lax.rsqrt(jnp.mean(values * values, -1, keepdims=True) + EPS)
        unit_rows = values * scale
        weighted = grad * gain
        inner = jnp.mean(weighted * unit_rows, -1, keepdims=True)
        gain_out[...] = jnp.sum(grad * unit_rows, 0, keepdims=True)
        total = scale * (weighted - unit_rows * inner) + up_ref[...].astype(F32)
        grad_out[...] = total
        sent_out[...] = total.astype(BF16)

    count = pl.num_programs(0)
    group = gathered.shape[2]
    for step, ref in enumerate(weight_refs):
        width = ref.shape[0]
        first = jnp.bitwise_xor(places_ref[1], step) * (width * count) + step_id * width
        whose = jnp.bitwise_xor(first // group, places_ref[0])
        at = pl.multiple_of(first % group, 128) if width < group else 0
        gathered[whose, :, pl.ds(at, width)] = mm(sent_out[...], ref[...], ROWS_ROWS).astype(BF16)

    @pl.when(step_id == count - 1)
    def _():
        for at, ref in enumerate(piece_outs):
            ref[...] = gathered[at]


def unmerge(places, gain, middle, upstream, grads, weights, pieces):
    rows, width = middle.shape
    parts = len(weights)
    depth = grads[0].shape[2]
    group = VD // pieces
    tile = min(weights[0].shape[0], group)
    whole = pl.BlockSpec((rows, width), lambda j, place: (0, 0))
    one_row = pl.BlockSpec((1, width), lambda j, place: (0, 0))
    return pl.pallas_call(
        functools.partial(unmerge_kernel, parts, pieces),
        grid_spec=pltpu.PrefetchScalarGridSpec(
            num_scalar_prefetch=1,
            grid=(weights[0].shape[0] // tile,),
            in_specs=[one_row, whole, whole]
            + [pl.BlockSpec((parts, rows, depth), lambda j, place: (0, 0, 0))] * parts
            + [pl.BlockSpec((tile, width), lambda j, place: (j, 0))] * parts,
            out_specs=[whole, whole, one_row]
            + [pl.BlockSpec((rows, group), lambda j, place: (0, 0))] * pieces,
            scratch_shapes=[pltpu.VMEM((pieces, rows, group), BF16)],
        ),
        out_shape=[
            jax.ShapeDtypeStruct((rows, width), F32),
            jax.ShapeDtypeStruct((rows, width), BF16),
            jax.ShapeDtypeStruct((1, width), F32),
        ]
        + [jax.ShapeDtypeStruct((rows, group), BF16)] * pieces,
        compiler_params=pltpu.CompilerParams(vmem_limit_bytes=VMEM_LIMIT),
        name="split_heads",
    )(places, gain, middle, upstream, *grads, *weights)


def outer_kernel(parts, places_ref, *refs):
    left_refs, right_refs, out_refs = refs[:parts], refs[parts : 2 * parts], refs[2 * parts :]
    total = None
    for left, right in zip(left_refs, right_refs):
        term = mm(left[...], right[...], COLS_COLS)
        total = term if total is None else total + term
    (out_ref,) = out_refs
    chunks, several, height, _ = out_ref.shape
    for one in range(several):
        for at in range(chunks):
            first = (one * chunks + at) * height
            out_ref[at, one] = total[first : first + height].astype(out_ref.dtype)


def outer_products(places, lefts, own_right, rights, owners, chunks):
    rows, width = lefts[0].shape
    parts = len(lefts)
    columns = own_right.shape[1] // parts
    own = width // owners
    tile = max(own, 256)
    fixed = pl.BlockSpec((rows, columns), lambda j, place: (0, 0))
    return pl.pallas_call(
        functools.partial(outer_kernel, parts),
        grid_spec=pltpu.PrefetchScalarGridSpec(
            num_scalar_prefetch=1,
            grid=(width // tile,),
            in_specs=[pl.BlockSpec((rows, tile), lambda j, place: (0, j))] * parts
            + [pl.BlockSpec((rows, columns), lambda j, place: (0, place[1]))]
            + [fixed] * (parts - 1),
            out_specs=pl.BlockSpec(
                (chunks, tile // own, own // chunks, columns), lambda j, place: (0, j, 0, 0)
            ),
        ),
        out_shape=jax.ShapeDtypeStruct((chunks, owners, own // chunks, columns), BF16),
        compiler_params=pltpu.CompilerParams(vmem_limit_bytes=VMEM_LIMIT),
        name="outer_products",
    )(places, *lefts, own_right, *rights)


def rows_kernel(pieces, places_ref, *refs):
    left_refs, right_refs, out_ref, left, right = (
        refs[:pieces], refs[pieces : 2 * pieces], refs[2 * pieces], refs[-2], refs[-1],
    )
    rows = left_refs[0].shape[0]

    @pl.when(pl.program_id(0) == 0)
    def _():
        for at, ref in enumerate(left_refs):
            left[at * rows : (at + 1) * rows] = ref[...]

    for at, ref in enumerate(right_refs):
        right[at * rows : (at + 1) * rows] = ref[...]
    parts, height, _ = out_ref.shape
    for step in range(parts):
        first = pl.multiple_of(jnp.bitwise_xor(places_ref[1], step) * height, 128)
        out_ref[step] = mm(left[:, pl.ds(first, height)], right[...], COLS_COLS).astype(
            out_ref.dtype
        )


def own_rows(places, lefts, rights, parts):
    pieces = len(lefts)
    rows, columns = lefts[0].shape
    height = columns // parts
    width = rights[0].shape[1]
    tile = 512
    return pl.pallas_call(
        functools.partial(rows_kernel, pieces),
        grid_spec=pltpu.PrefetchScalarGridSpec(
            num_scalar_prefetch=1,
            grid=(width // tile,),
            in_specs=[pl.BlockSpec((rows, columns), lambda j, place: (0, 0))] * pieces
            + [pl.BlockSpec((rows, tile), lambda j, place: (0, j))] * pieces,
            out_specs=pl.BlockSpec((parts, height, tile), lambda j, place: (0, 0, j)),
            scratch_shapes=[
                pltpu.VMEM((pieces * rows, columns), BF16),
                pltpu.VMEM((pieces * rows, tile), BF16),
            ],
        ),
        out_shape=jax.ShapeDtypeStruct((parts, height, width), BF16),
        compiler_params=pltpu.CompilerParams(vmem_limit_bytes=VMEM_LIMIT),
        name="own_rows",
    )(places, *lefts, *rights)


def again_kernel(parts, places_ref, normed_ref, up_ref, *refs):
    gate_refs, wide_refs, down_ref = refs[:parts], refs[parts : 2 * parts], refs[2 * parts]
    hidden_ref, gate_out, wide_out = refs[-3:]
    depth = gate_refs[0].shape[0]
    gate, wide = None, None
    for step in range(parts):
        first = pl.multiple_of(jnp.bitwise_xor(places_ref[1], step) * depth, 128)
        left = normed_ref[:, pl.ds(first, depth)]
        one, two = mm(left, gate_refs[step][...]), mm(left, wide_refs[step][...])
        gate, wide = (one, two) if gate is None else (gate + one, wide + two)
    hidden_grad = mm(up_ref[...], down_ref[...], ROWS_ROWS)
    slope = jax.nn.sigmoid(gate)
    hidden_ref[...] = (gate * slope * wide).astype(BF16)
    gate_out[...] = (hidden_grad * wide * (slope * (1.0 + gate * (1.0 - slope)))).astype(BF16)
    wide_out[...] = (hidden_grad * gate * slope).astype(BF16)


def feed_again(places, normed, upstream, gates, wides, down, step, before=()):
    count, width = normed.shape
    parts = len(gates)
    depth, columns = gates[0].shape
    tile = 256
    tiles = count // tile
    there = lambda j, place: (jnp.bitwise_xor(place[1], step) * tiles + j, 0)
    here = lambda j, place: (j, 0)
    fixed = pl.BlockSpec((depth, columns), lambda j, place: (0, 0))
    carried = 1 + 2 + 2 * parts + 1
    return pl.pallas_call(
        functools.partial(again_kernel, parts),
        grid_spec=pltpu.PrefetchScalarGridSpec(
            num_scalar_prefetch=1,
            grid=(tiles,),
            in_specs=[pl.BlockSpec((tile, width), here), pl.BlockSpec((tile, width), there)]
            + [fixed] * (2 * parts)
            + [pl.BlockSpec((columns, width), lambda j, place: (0, 0))]
            + [pl.BlockSpec(memory_space=pl.ANY)] * len(before),
            out_specs=[pl.BlockSpec((tile, columns), there)]
            + [pl.BlockSpec((tile, columns), here)] * 2,
        ),
        out_shape=[
            jax.ShapeDtypeStruct((upstream.shape[0], columns), BF16),
            jax.ShapeDtypeStruct((count, columns), BF16),
            jax.ShapeDtypeStruct((count, columns), BF16),
        ],
        input_output_aliases={carried + at: at for at in range(len(before))},
        compiler_params=pltpu.CompilerParams(vmem_limit_bytes=VMEM_LIMIT),
        name="feed_again",
    )(places, normed, upstream, *gates, *wides, down, *before)


def place_in_kernel(columns_of, head_of, in_ref, out_ref, held, sems):
    step_id = pl.program_id(0)
    slot = lax.rem(step_id, 2)

    def copies(which, where):
        found = []
        for number, (low, width, first) in enumerate(columns_of):
            at = pl.multiple_of(first + head_of(which) * width, 128)
            found.append(
                pltpu.make_async_copy(
                    held.at[where, :, pl.ds(low, width)],
                    out_ref.at[:, pl.ds(at, width)],
                    sems.at[where, number],
                )
            )
        return found

    @pl.when(step_id >= 2)
    def _():
        for copy in copies(step_id - 2, slot):
            copy.wait()

    held[slot] = in_ref[:, 0].astype(F32).reshape(held.shape[1:])
    for copy in copies(step_id, slot):
        copy.start()

    @pl.when(step_id == pl.num_programs(0) - 1)
    def _():
        for copy in copies(step_id - 1, 1 - slot) + copies(step_id, slot):
            copy.wait()


def place_in(value, seqs):
    blocks, sources, rows, columns = value.shape
    heads = HEADS // seqs
    per_source = columns // HEAD_WIDTH
    columns_of = [(0, DK, 0), (DK, DK, KD), (2 * DK, DV, 2 * KD), (2 * DK + DV, DV, CONVW)]

    def head_of(step):
        source = step // per_source
        return source % seqs * heads + source // seqs * per_source + step % per_source

    return pl.pallas_call(
        functools.partial(place_in_kernel, columns_of, head_of),
        grid=(sources * per_source,),
        in_specs=[
            pl.BlockSpec(
                (blocks, 1, rows, HEAD_WIDTH), lambda h: (0, h // per_source, 0, h % per_source)
            )
        ],
        out_specs=pl.BlockSpec(memory_space=pl.ANY),
        out_shape=jax.ShapeDtypeStruct((blocks * rows, PROJW), F32),
        scratch_shapes=[
            pltpu.VMEM((2, blocks * rows, HEAD_WIDTH), F32),
            pltpu.SemaphoreType.DMA((2, len(columns_of))),
        ],
        compiler_params=pltpu.CompilerParams(vmem_limit_bytes=VMEM_LIMIT),
        name="place_w_in",
    )(value)


def place_gu_kernel(half, gate_ref, wide_ref, out_ref):
    def put(ref):
        width = ref.shape[2]
        for at in range(ref.shape[0]):
            out_ref[:, at * width : (at + 1) * width] = ref[at].astype(F32)

    @pl.when(pl.program_id(0) < half)
    def _():
        put(gate_ref)

    @pl.when(pl.program_id(0) >= half)
    def _():
        put(wide_ref)


def place_gu(gate, wide):
    sources, rows, width = gate.shape
    together = 1
    while together * width % 128:
        together *= 2
    half = sources // together
    return pl.pallas_call(
        functools.partial(place_gu_kernel, half),
        grid=(2 * half,),
        in_specs=[
            pl.BlockSpec((together, rows, width), lambda j: (jnp.minimum(j, half - 1), 0, 0)),
            pl.BlockSpec((together, rows, width), lambda j: (jnp.maximum(j - half, 0), 0, 0)),
        ],
        out_specs=pl.BlockSpec((rows, together * width), lambda j: (0, j)),
        out_shape=jax.ShapeDtypeStruct((rows, 2 * sources * width), F32),
        compiler_params=pltpu.CompilerParams(vmem_limit_bytes=VMEM_LIMIT),
        name="place_w_gu",
    )(gate, wide)


def line_first(value):
    return lax.ppermute(value, "replica", [(0, 1), (3, 2)])


def line_second(value):
    return lax.ppermute(value, "replica", [(1, 2), (2, 1)])


def line_third(value):
    return lax.ppermute(value, "replica", [(1, 0), (2, 3)])


def added(left, right):
    return (left.astype(F32) + right.astype(F32)).astype(BF16)


def pinned(*values):
    return lax.optimization_barrier(values)


def line_sum(value):
    value = added(value, line_first(value))
    value = added(value, line_second(value))
    return settled_pair((value, line_third(value)))


def settled_pair(pair):
    place = lax.axis_index("replica")
    return jnp.where((place == 1) | (place == 2), pair[0], pair[1]).astype(F32)


def swapped(value, axis, step):
    count = lax.axis_size(axis)
    return lax.ppermute(value, axis, [(source, source ^ step) for source in range(count)])


def around(value, axis):
    return [value] + [swapped(value, axis, step) for step in range(1, lax.axis_size(axis))]


def settled(parts, index):
    stacked = jnp.stack(parts)
    return [
        lax.dynamic_index_in_dim(stacked, jnp.bitwise_xor(index, at), 0, keepdims=False)
        for at in range(len(parts))
    ]


def part_of(value, index, count, axis):
    width = value.shape[axis] // count
    return lax.dynamic_slice_in_dim(value, index * width, width, axis)


def dot(left, right):
    return jnp.dot(left, right, preferred_element_type=F32)


def dot_rows(left, right):
    return lax.dot_general(left, right, (((1,), (1,)), ((), ())), preferred_element_type=F32)


def dot_cols(left, right):
    return lax.dot_general(left, right, (((0,), (0,)), ((), ())), preferred_element_type=F32)


def rms_parts(values):
    return lax.rsqrt(jnp.mean(values * values, -1, keepdims=True) + EPS)


def rms_back(values, scale, gain, grad):
    weighted = grad * gain
    unit_rows = values * scale
    inner = jnp.mean(weighted * unit_rows, -1, keepdims=True)
    return scale * (weighted - unit_rows * inner), jnp.sum(grad * unit_rows, 0)


def body(
    tokens,
    cotangent,
    lengths,
    norm_gains,
    w_in,
    w_ab,
    conv_weight,
    gate_params,
    onorm_gain,
    w_o,
    w_gu,
    w_down,
):
    shards, seqs, replicas = (lax.axis_size(name) for name in EVERY)
    shard, seq = lax.axis_index("shard"), lax.axis_index("seq")
    owners = shards * seqs
    owner = shard * seqs + seq
    micro, row = tokens.shape[0], tokens.shape[1]
    flat = micro * row
    length = row * seqs
    heads = HEADS // seqs
    depth = D // shards
    seq_place = jnp.reshape(seq, (1,)).astype(jnp.int32)
    shard_place = jnp.reshape(shard, (1,)).astype(jnp.int32)
    places = jnp.stack([seq, shard]).astype(jnp.int32)

    def blocks(value, count, axis=1):
        return [part_of(value, jnp.bitwise_xor(shard, step), count, axis) for step in range(count)]

    flat_tokens = tokens.reshape(flat, D)
    in_own = pick_heads(seq_place, w_in, heads)
    sent_tokens, in_own = pinned(flat_tokens, in_own)
    pieces = around(sent_tokens, "seq")
    gain_parts = around(norm_gains, "shard")
    in_parts = around(in_own, "shard")
    taps_parts = around(conv_weight, "shard")
    ab_parts = around(w_ab, "shard")
    gains = jnp.concatenate(settled(gain_parts, shard), 1).astype(F32)
    gain_first, gain_second = gains[:1], gains[1:]
    taps = jnp.concatenate(settled(taps_parts, shard), 1)
    upstream = cotangent.reshape(flat, D)
    up_parts = around(upstream, "shard")
    hidden_grad = dot_rows(jnp.concatenate(up_parts, 0), w_down)
    own_out, own_gu, late_up, hidden_grad, *arrived = pinned(
        w_o, w_gu, upstream, hidden_grad, *pieces, *in_parts
    )
    pieces, in_parts = arrived[:seqs], arrived[seqs:]
    all_up = lax.all_gather(late_up, EVERY, axis=0, tiled=True)
    out_parts = around(own_out, "shard")
    gu_parts = around(own_gu, "shard")

    normed, projected = project(shard_place, gain_first, pieces, in_parts)
    rate_in = sum(dot(left, right) for left, right in zip(blocks(normed, shards), ab_parts))
    rate_in = part_of(rate_in.reshape(seqs, micro, row, 2, HEADS), seq, seqs, 4)
    rate_in = jnp.stack(settled(list(rate_in), seq))
    rate_in = jnp.transpose(rate_in, (3, 1, 4, 0, 2)).reshape(2, micro, heads, length)
    position = jnp.arange(length, dtype=jnp.int32)
    valid = (position[None, :] < lengths[:, None]).astype(F32)[:, None, :]
    own_params = part_of(gate_params, seq, seqs, 1)[:, None, :, None]
    rate_shifted = rate_in[0] + own_params[1]
    decays = -jnp.exp(own_params[0]) * jax.nn.softplus(rate_shifted) * valid
    written = jax.nn.sigmoid(rate_in[1])
    rates = jnp.stack([jnp.maximum(decays, LOWEST_DECAY), written * valid], 2)
    rates = jnp.pad(rates, ((0, 0), (0, 0), (0, SMALL_ROWS - 2), (0, 0)))
    gain_row = onorm_gain.reshape(1, DV)
    projected = projected.reshape(seqs, micro, row, -1)
    *gated, inverse, update = mixer_forward(seq_place, projected, taps, rates, gain_row, 2)
    gated = [item.reshape(flat, heads * DV) for item in gated]

    mixed_parts = [gated[0]] + [swapped(gated[step], "seq", step) for step in range(1, seqs)]
    arrived = pinned(*mixed_parts, *gu_parts)
    mixed_parts, gu_parts = list(arrived[:seqs]), list(arrived[seqs:])

    middle, renormed, *mixed_left = merge(
        places, gain_second, flat_tokens, mixed_parts, out_parts
    )
    line_renormed = lax.all_gather(renormed, "replica", axis=0, tiled=True)

    mixed_left = [
        swapped(item, "seq", step) if step else item for step, item in enumerate(mixed_left)
    ]
    fed = feed(places, around(renormed, "shard"), hidden_grad, gu_parts)
    fed = pinned(*fed, *mixed_left)
    fed, mixed_left = fed[: shards + 1], fed[shards + 1 :]
    grads_back = [fed[0]] + [swapped(fed[step], "shard", step) for step in range(1, shards)]
    middle_grad, mixed_grad, gain2_grad, *gated_grad = unmerge(
        places, gain_second, middle, upstream, grads_back, out_parts, seqs
    )
    hidden = fed[shards]

    ff_own = FF // owners
    own_down = part_of(w_down, seq, seqs, 0)
    own_gate = [part_of(part, owner, 2 * owners, 1) for part in gu_parts]
    own_wide = [part_of(part, owners + owner, 2 * owners, 1) for part in gu_parts]

    gated_grad = [
        swapped(item, "seq", step) if step else item for step, item in enumerate(gated_grad)
    ]
    all_up, mixed_grad, own_down, *others = pinned(
        all_up, mixed_grad, own_down, *own_gate, *own_wide, *gated_grad
    )
    own_gate, own_wide = others[:shards], others[shards : 2 * shards]
    gated_grad = others[2 * shards :]
    gated_grad = [item.reshape(micro, row, heads * DV) for item in gated_grad]
    mid_pieces = around(mixed_grad, "seq")
    proj_grad, small_grad = mixer_backward(
        seq_place, projected, taps, rates, gain_row, inverse, update, gated_grad, 1
    )
    proj_grad, *mid_pieces = pinned(proj_grad, *mid_pieces)
    rows_all = seqs * flat
    proj_grad = proj_grad.reshape(rows_all, -1)
    pair_proj = [
        swapped(part_of(proj_grad, jnp.bitwise_xor(shard, step), shards, 1), "shard", step)
        for step in range(1, shards)
    ]

    pair_normed = around(normed, "shard")
    spread = jnp.broadcast_to(line_renormed[None], (seqs,) + line_renormed.shape)
    spread, *pair_proj = pinned(spread, *pair_proj)
    grad_in = outer_products(places, pair_normed, proj_grad, pair_proj, owners, replicas)
    width = grad_in.shape[3]
    proj_grad, small_grad, grad_in, spread, *mid_pieces = pinned(
        proj_grad, small_grad, grad_in, spread, *mid_pieces
    )
    grad_in = lax.psum_scatter(grad_in, "replica", scatter_dimension=0, tiled=False)
    own_renormed = lax.all_to_all(spread, "seq", split_axis=0, concat_axis=0).reshape(-1, D)

    grad_out = own_rows(places, mixed_left, mid_pieces, shards)
    grad_out = functools.reduce(
        added, [grad_out[0]] + [swapped(grad_out[step], "shard", step) for step in range(1, shards)]
    )

    def input_gradient_parts(proj_grad, small_grad):
        decay_grad = small_grad[:, :, 5, :length]
        write_grad = small_grad[:, :, 6, :length]
        shifted_grad = decay_grad * -jnp.exp(own_params[0]) * jax.nn.sigmoid(rate_shifted) * valid
        params_grad = jnp.stack(
            [jnp.sum(decay_grad * decays, (0, 2)), jnp.sum(shifted_grad, (0, 2))]
        )
        rate_grad = jnp.stack([shifted_grad, write_grad * written * (1.0 - written) * valid])
        rate_grad = jnp.transpose(rate_grad.reshape(2, micro, heads, seqs, row), (3, 1, 4, 0, 2))
        rate_grad = jnp.stack(settled(list(rate_grad), seq))
        rate_grad = rate_grad.reshape(rows_all, 2 * heads)
        grad_ab = lax.dot_general(
            rate_grad, normed.astype(F32), (((0,), (0,)), ((), ())), precision=HIGHEST
        )
        own_ab = [
            part_of(part.reshape(depth, 2, HEADS), seq, seqs, 2).reshape(depth, 2 * heads)
            for part in ab_parts
        ]
        normed_grad = [
            dot_rows(proj_grad, part)
            + lax.dot_general(
                rate_grad, ab.astype(F32), (((1,), (1,)), ((), ())), precision=HIGHEST
            )
            for part, ab in zip(in_parts, own_ab)
        ]
        return (*normed_grad, grad_ab, params_grad)

    def input_gradient(*normed_grad):
        *normed_grad, grad_ab, params_grad = normed_grad
        normed_grad = jnp.concatenate(settled(normed_grad, shard), 1).reshape(seqs, flat, D)
        normed_grad = normed_grad[0] + sum(
            swapped(normed_grad[step].astype(BF16), "seq", step).astype(F32)
            for step in range(1, seqs)
        )
        flat_in = flat_tokens.astype(F32)
        inputs_grad, gain1_grad = rms_back(flat_in, rms_parts(flat_in), gains[0], normed_grad)
        input_grads = (inputs_grad + middle_grad).astype(BF16).reshape(micro, row, D)
        return input_grads, gain1_grad, grad_ab, params_grad

    def to_group(value):
        return lax.all_to_all(value, GROUP, split_axis=0, concat_axis=0, tiled=False)

    def to_owners(value):
        return to_group(value.astype(BF16).reshape(owners, D // owners, ff_own))

    normed_parts = input_gradient_parts(proj_grad, small_grad)
    replica = lax.axis_index("replica")
    grad_out = [
        swapped(part_of(grad_out, jnp.bitwise_xor(replica, step), replicas, 0), "replica", step)
        if step
        else part_of(grad_out, replica, replicas, 0)
        for step in range(replicas)
    ]
    own_renormed, *normed_parts = pinned(own_renormed, *normed_parts)
    input_grads, gain1_grad, grad_ab, params_grad = input_gradient(*normed_parts)
    gain2_grad = gain2_grad[0]
    all_renormed = around(own_renormed, "shard")

    def again(at, before=()):
        return feed_again(
            places, all_renormed[at], all_up, own_gate, own_wide, own_down, at, before
        )

    def over_tokens(lefts, rights):
        return sum(dot_cols(left, right) for left, right in zip(lefts, rights))

    parts = [again(0)]
    input_grads, gain1_grad, grad_ab, params_grad, *others = pinned(
        input_grads, gain1_grad, grad_ab, params_grad, *grad_out, *parts[0]
    )
    grad_out, parts[0] = others[:replicas], others[replicas:]
    grad_out = sum(item.astype(F32) for item in grad_out).astype(BF16)
    taps_grad = jnp.sum(small_grad[:, :, :KERNEL], 0)
    conv_grad = jnp.concatenate(
        [
            jnp.swapaxes(taps_grad[..., low:high], 0, 1).reshape(KERNEL, -1)
            for low, high in ((0, DK), (DK, 2 * DK), (2 * DK, 2 * DK + DV))
        ],
        1,
    )
    onorm_grad = jnp.sum(small_grad[:, :, 4, :DV], (0, 1))
    loose = jnp.concatenate([onorm_grad, params_grad.reshape(-1)])
    loose = jnp.pad(loose, (0, D - loose.size))
    rows_ab = 2 * heads
    smalls = jnp.concatenate(
        [grad_ab, conv_grad, loose[None], gain1_grad[None], gain2_grad[None]], 0
    )
    step = 1
    while step < shards:
        smalls = smalls + swapped(smalls, "shard", step)
        step *= 2
    rows_small = smalls.shape[0]
    high = lax.optimization_barrier(smalls.astype(BF16))
    low = (smalls - high.astype(F32)).astype(BF16)
    fill = jnp.zeros((-(2 * rows_small) % 16, D), BF16)
    rows_own = grad_out.shape[0]
    grad_out = jnp.concatenate([grad_out, high, low, fill], 0)
    grad_out, *all_renormed = pinned(grad_out, *all_renormed)
    grad_out = lax.all_gather(grad_out, "replica", axis=0)
    for at in range(1, shards):
        parts.append(again(at, parts[-1][:1]))
    grad_in, hidden, own_hidden = pinned(grad_in, hidden, parts[-1][0])
    grad_in = to_group(grad_in)
    gate_grad, wide_grad = ([part[which] for part in parts] for which in (1, 2))
    grad_gate = over_tokens(all_renormed, gate_grad).astype(BF16)
    grad_in, grad_gate, own_hidden, *wide_grad = pinned(
        grad_in, grad_gate, own_hidden, *wide_grad
    )
    grad_in = lax.all_gather(grad_in, "replica", axis=0)
    grad_gate = to_owners(grad_gate)
    grad_wide = over_tokens(all_renormed, wide_grad).astype(BF16)
    grad_down = dot_cols(own_hidden, all_up)
    grad_wide, grad_gate, grad_out = pinned(grad_wide, grad_gate, grad_out)
    grad_wide = to_owners(grad_wide)
    rows_down = dot(hidden, w_down).reshape(shards, flat, D)
    result = (
        middle
        + rows_down[0]
        + sum(swapped(rows_down[step], "shard", step) for step in range(1, shards))
    )
    results = result.astype(BF16).reshape(micro, row, D)
    smalls = grad_out[:, rows_own : rows_own + 2 * rows_small].astype(F32)
    smalls = jnp.sum(smalls[:, :rows_small] + smalls[:, rows_small:], 0)
    grad_out = grad_out[:, :rows_own].reshape(replicas * rows_own, D).astype(F32)
    every = jnp.stack(settled(around(smalls, "seq"), seq))
    grad_gu = place_gu(grad_gate, grad_wide)
    if width % HEAD_WIDTH == 0:
        grad_in = place_in(grad_in, seqs)
    else:
        grad_in = grad_in.reshape(replicas, shards, seqs, -1, width)
        grad_in = jnp.transpose(grad_in, (0, 3, 2, 1, 4)).reshape(D // owners, HEADS, HEAD_WIDTH)
        cuts = (0, DK, 2 * DK, 2 * DK + DV, HEAD_WIDTH)
        grad_in = jnp.concatenate(
            [
                grad_in[..., low:high].reshape(D // owners, -1)
                for low, high in zip(cuts[:-1], cuts[1:])
            ],
            1,
        ).astype(F32)

    ab_total = jnp.transpose(every[:, :rows_ab].reshape(seqs, 2, heads, D), (3, 1, 0, 2))
    ab_total = ab_total.reshape(D, 2 * HEADS)
    conv_all = every[:, rows_ab : rows_ab + KERNEL]
    conv_total = jnp.concatenate(
        [
            jnp.swapaxes(conv_all[..., low:high], 0, 1).reshape(KERNEL, -1)
            for low, high in (
                (0, heads * DK),
                (heads * DK, 2 * heads * DK),
                (2 * heads * DK, heads * (2 * DK + DV)),
            )
        ],
        1,
    )
    loose_all = every[:, rows_ab + KERNEL]
    onorm_total = jnp.sum(loose_all[:, :DV], 0)
    params_total = loose_all[:, DV : DV + 2 * heads].reshape(seqs, 2, heads)
    params_total = jnp.swapaxes(params_total, 0, 1).reshape(2, HEADS)
    gains_total = jnp.sum(every[:, rows_ab + KERNEL + 1 : rows_ab + KERNEL + 3], 0)
    gains_own = part_of(gains_total, owner, owners, 1)
    ab_own = part_of(ab_total, owner, owners, 0)
    conv_own = part_of(conv_total, owner, owners, 1)
    return (
        results,
        input_grads,
        gains_own,
        grad_in,
        ab_own,
        conv_own,
        params_total,
        onorm_total,
        grad_out,
        grad_gu,
        grad_down,
    )


def solution(mesh):
    in_specs = (
        P(("shard", "replica"), "seq", None),
        P(("shard", "replica"), "seq", None),
        P(("shard", "replica")),
        P(None, "shard"),
        P("shard", None),
        P("shard", None),
        P(None, "shard"),
        P(),
        P(),
        P("shard", None),
        P("shard", None),
        P("shard", None),
    )
    out_specs = (
        P(("shard", "replica"), "seq", None),
        P(("shard", "replica"), "seq", None),
        P(None, ("shard", "seq")),
        P(("shard", "seq"), None),
        P(("shard", "seq"), None),
        P(None, ("shard", "seq")),
        P(),
        P(),
        P(("shard", "seq"), None),
        P(("shard", "seq"), None),
        P(("shard", "seq"), None),
    )
    return jax.shard_map(body, mesh=mesh, in_specs=in_specs, out_specs=out_specs, check_vma=False)
```

profile of v0, /device:TPU:0, one launch (start us, length us, event | category | flops | bytes accessed | tf_op | source)
XLA Modules:
  0.0 654.5 jit_solution(7327550114581707240)
XLA Ops:
  7.3 6.1 pick_heads.1.refs_4_
  13.9 2.9 collective-permute-start.2
  18.4 3.0 collective-permute-done.1
  21.4 9.0 %fusion.10.refs_2_ = f32[256,2816]{1,0:T(8,128)} fusion(bf16[2816,2048]{1,0:T(8,128)(2,1)} %param.23, bf16[128,2048]{1,0:T(8,128)(2,1)S(1)} %collective-permute-done.1, bf16[128,2048]{1,0:T(8,128)(2,1)S(1)} %bitcast.185), kind=kOutput, calls=%fused_computation.29 | convolution fusion | flops 2954887168 | bytes 15466496 | tf_op jit(solution)/shard_map/dot_general | solution.py:991
  30.5 11.3 %collective-permute-done.3.refs_2_ = bf16[128,2048]{1,0:T(8,128)(2,1)S(1)} collective-permute-done((bf16[128,2048]{1,0:T(8,128)(2,1)S(1)}, bf16[128,2048]{1,0:T(8,128)(2,1)S(1)}, u32[]{:S(2)}, u32[]{:S(2)}) %collective-permute-start.3) | collective-permute-done | bytes 524320 | tf_op jit(solution)/shard_map/ppermute | solution.py:966
  43.2 5.4 collective-permute-done
  50.0 12.9 %project.1 = (bf16[512,2048]{1,0:T(8,128)(2,1)}, f32[512,3072]{1,0:T(8,128)}) custom-call(s32[1]{0:T(128)} %bitcast.1.place_ref, f32[1,2048]{1,0:T(1,128)} %get-tuple-element.282.gain_ref, bf16[128,2048]{1,0:T(8,128)(2,1)} %bitcast.164, bf16[128,2048]{1,0:T(8,128)(2,1)} %copy-done.18, bf16[128,2048]{1,0:T(8,128)(2,1)} %copy-done.19, ...), custom_call_target="tpu_custom_call" | custom-call | tf_op jit(solution)/shard_map/project/pallas_call | solution.py:433
  67.5 22.4 %mixer_forward.1 = (bf16[2,64,1024]{2,1,0:T(8,128)(2,1)}, bf16[2,64,1024]{2,1,0:T(8,128)(2,1)}, bf16[2,64,1024]{2,1,0:T(8,128)(2,1)}, bf16[2,64,1024]{2,1,0:T(8,...) custom-call(s32[1]{0:T(128)} %bitcast.place_ref, f32[4,2,64,3072]{3,2,1,0:T(8,128)} %bitcast.162, ...), custom_call_target="tpu_custom_call" | custom-call | tf_op jit(solution)/shard_map/mixer_forward/pallas_call | solution.py:323
  94.1 6.2 collective-permute-done.10.refs_3_
  100.3 5.1 collective-permute-done.8.refs_1_
  106.3 11.1 %merge_heads.1 = (f32[128,2048]{1,0:T(8,128)}, bf16[128,2048]{1,0:T(8,128)(2,1)}, bf16[128,1024]{1,0:T(8,128)(2,1)}, bf16[128,1024]{1,0:T(8,128)(2,1)}, bf16[128...) custom-call(s32[2]{0:T(128)} %pad_add_fusion.places_ref, f32[1,2048]{1,0:T(1,128)} %get-tuple-element.281.gain_ref, ...), custom_call_target="tpu_custom_call" | custom-call | tf_op jit(solution)/shard_map/merge_heads/pallas_call | solution.py:509
  121.7 21.9 %feed_forward.1 = (f32[2,128,1024]{2,1,0:T(8,128)}, f32[2,128,1024]{2,1,0:T(8,128)}, bf16[256,2816]{1,0:T(8,128)(2,1)}) custom-call(s32[2]{0:T(128)} %pad_add_fusion.places_ref, bf16[128,2048]{1,0:T(8,128)(2,1)} %get-tuple-element.148.refs_0_, bf16[128,2048]{1,0:T(8,128)(2,1)} %copy-done.17, f32[256,2816]{1,0:T(8,128)} %fusion.10.refs_2_, ...), custom_call_target="tpu_custom_call" | custom-call | tf_op jit(solution)/shard_map/feed_forward/pallas_call | solution.py:601
  145.6 3.8 constant_dynamic-slice_fusion.19.refs_4_
  150.4 13.4 %split_heads.1 = (f32[128,2048]{1,0:T(8,128)}, bf16[128,2048]{1,0:T(8,128)(2,1)}, f32[1,2048]{1,0:T(1,128)}, bf16[128,1024]{1,0:T(8,128)(2,1)}, bf16[128,1024]{1...) custom-call(s32[2]{0:T(128)} %pad_add_fusion.places_ref, f32[1,2048]{1,0:T(1,128)} %get-tuple-element.281.gain_ref, ...), custom_call_target="tpu_custom_call" | custom-call | tf_op jit(solution)/shard_map/split_heads/pallas_call | solution.py:679
  167.2 9.5 %constant_dynamic-slice_fusion.15 = (bf16[1024,704]{1,0:T(8,128)(2,1)}, bf16[1024,704]{1,0:T(8,128)(2,1)}, bf16[1024,704]{1,0:T(8,128)(2,1)}, bf16[1024,704]{1,0:T(8,128)(2,1)}) fusion(bf16[1024,11264]{1,0:T(8,128)(2,1)} %collective-permute-done.11.refs_4_.refs_6_, s32[]{:T(128)S(6)} %select_n.120, s32[]{:T(128)S(6)} %select_n.119, bf16[1024,11264]{1,0:T(8,128)(2,1)} %refs_5_), kind=kLoop, calls=%fused_computation.107 | loop fusion | bytes 11534344 | tf_op jit(solution)/shard_map/dynamic_slice | solution.py:983
  183.1 20.3 %mixer_backward.1 = (bf16[4,2,64,3072]{3,2,1,0:T(8,128)(2,1)}, f32[2,4,8,512]{3,2,1,0:T(8,128)}) custom-call(s32[1]{0:T(128)} %bitcast.place_ref, f32[4,2,64,3072]{3,2,1,0:T(8,128)} %bitcast.163, bf16[4,8192]{1,0:T(4,128)(2,1)} %pad_maximum_fusion.3.taps_q.taps_k.taps_v, bf16[4,8192]{1,0:T(4,128)(2,1)} %pad_maximum_fusion.3.taps_q.taps_k.taps_v, ...), custom_call_target="tpu_custom_call" | custom-call | tf_op jit(solution)/shard_map/mixer_backward/pallas_call | solution.py:349
  208.3 6.3 all-gather.9.cloned.1.call-done
  214.7 6.1 broadcast_in_dim.8
  220.8 12.8 %outer_products.1 = bf16[4,8,64,1536]{3,2,1,0:T(8,128)(2,1)} custom-call(s32[2]{0:T(128)} %pad_add_fusion.places_ref, bf16[512,2048]{1,0:T(8,128)(2,1)} %get-tuple-element.133.refs_0_, bf16[512,2048]{1,0:T(8,128)(2,1)} %collective-permute-done.24.refs_1_, bf16[512,3072]{1,0:T(8,128)(2,1)} %bitcast.172, bf16[512,1536]{1,0:T(8,128)(2,1)} %collective-permute-done.25.refs_3_), custom_call_target="tpu_custom_call" | custom-call | tf_op jit(solution)/shard_map/outer_products/pallas_call | solution.py:723
  233.5 5.6 all-to-all-start
  244.9 6.2 convolution_add_fusion
  251.1 4.8 convolution_add_fusion.1
  255.9 75.9 %all-to-all-done = bf16[4,512,2048]{2,1,0:T(8,128)(2,1)} async-done(((bf16[4,512,2048]{2,1,0:T(8,128)(2,1)}), bf16[4,512,2048]{2,1,0:T(8,128)(2,1)}, u32[]{:S(2)}, u32[]{:S(2)}) %all-to-all-start) | async-done | bytes 8388640 | tf_op jit(solution)/shard_map/all_to_all | solution.py:1135
  331.8 7.1 %own_rows.1 = bf16[2,512,2048]{2,1,0:T(8,128)(2,1)} custom-call(s32[2]{0:T(128)} %pad_add_fusion.places_ref, bf16[128,1024]{1,0:T(8,128)(2,1)} %get-tuple-element.190.refs_0_, bf16[128,1024]{1,0:T(8,128)(2,1)} %copy-done.29, bf16[128,1024]{1,0:T(8,128)(2,1)} %copy-done.30, bf16[128,1024]{1,0:T(8,128)(2,1)} %copy-done.31, ...), custom_call_target="tpu_custom_call" | custom-call | tf_op jit(solution)/shard_map/own_rows/pallas_call | solution.py:768
  338.9 3.2 slice_bitcast_fusion
  343.1 2.7 fusion.5
  353.1 28.2 %feed_again.2 = (bf16[4096,704]{1,0:T(8,128)(2,1)}, bf16[2048,704]{1,0:T(8,128)(2,1)}, bf16[2048,704]{1,0:T(8,128)(2,1)}) custom-call(s32[2]{0:T(128)} %pad_add_fusion.places_ref, bf16[2048,2048]{1,0:T(8,128)(2,1)} %bitcast.27.normed_ref, bf16[4096,2048]{1,0:T(8,128)(2,1)} %all-gather.7.cloned.1.call-done.up_ref, ...), custom_call_target="tpu_custom_call" | custom-call | tf_op jit(solution)/shard_map/feed_again/pallas_call | solution.py:814
  388.7 30.4 %collective-permute-done.31 = bf16[128,2048]{1,0:T(8,128)(2,1)S(1)} collective-permute-done((bf16[128,2048]{1,0:T(8,128)(2,1)}, bf16[128,2048]{1,0:T(8,128)(2,1)S(1)}, u32[]{:S(2)}, u32[]{:S(2)}) %collective-permute-start.31) | collective-permute-done | bytes 524320 | tf_op jit(solution)/shard_map/ppermute | solution.py:966
  421.8 28.3 %feed_again.3 = (bf16[4096,704]{1,0:T(8,128)(2,1)}, bf16[2048,704]{1,0:T(8,128)(2,1)}, bf16[2048,704]{1,0:T(8,128)(2,1)}) custom-call(s32[2]{0:T(128)} %pad_add_fusion.places_ref, bf16[2048,2048]{1,0:T(8,128)(2,1)} %collective-permute-done.34.normed_ref, bf16[4096,2048]{1,0:T(8,128)(2,1)} %all-gather.7.cloned.1.call-done.up_ref, ...), custom_call_target="tpu_custom_call", output_to_operand_aliasing={{0}: (8, {})} | custom-call | tf_op jit(solution)/shard_map/feed_again/pallas_call | solution.py:814
  450.1 3.7 all-to-all-start.1
  454.5 6.2 fusion.56
  463.5 9.0 %fusion.57 = f32[2048,704]{0,1:T(8,128)S(1)} fusion(bf16[2048,2048]{1,0:T(8,128)(2,1)} %collective-permute-done.34.normed_ref, bf16[2048,704]{1,0:T(8,128)(2,1)S(1)} %copy-done.42), kind=kOutput, calls=%fused_computation.170 | convolution fusion | flops 5905580032 | bytes 17039360 | tf_op jit(solution)/shard_map/dot_general | solution.py:995
  472.6 10.3 %add_convert_fusion.1 = bf16[2048,704]{0,1:T(8,128)(2,1)} fusion(f32[2048,704]{0,1:T(8,128)S(1)} %fusion.57, bf16[2048,2048]{1,0:T(8,128)(2,1)} %bitcast.27.normed_ref, bf16[2048,704]{1,0:T(8,128)(2,1)S(1)} %copy-done.41), kind=kOutput, calls=%fused_computation.1 | convolution fusion | flops 5908463616 | bytes 19922944 | tf_op jit(solution)/shard_map/dot_general | solution.py:995
  484.2 2.8 fusion.9
  488.7 4.3 all-to-all-start.2
  493.1 11.3 %fusion.58 = f32[2048,704]{0,1:T(8,128)} fusion(bf16[2048,2048]{1,0:T(8,128)(2,1)} %collective-permute-done.34.normed_ref, bf16[2048,704]{1,0:T(8,128)(2,1)} %get-tuple-element.229), kind=kOutput, calls=%fused_computation.171 | convolution fusion | flops 5905580032 | bytes 17039360 | tf_op jit(solution)/shard_map/dot_general | solution.py:995
  504.4 12.3 %add_convert_fusion = bf16[2048,704]{0,1:T(8,128)(2,1)} fusion(f32[2048,704]{0,1:T(8,128)} %fusion.58, bf16[2048,2048]{1,0:T(8,128)(2,1)} %bitcast.27.normed_ref, bf16[2048,704]{1,0:T(8,128)(2,1)S(1)} %copy-done.40), kind=kOutput, calls=%fused_computation | convolution fusion | flops 5908463616 | bytes 19922944 | tf_op jit(solution)/shard_map/dot_general | solution.py:995
  516.7 16.7 %fusion.59 = f32[704,2048]{1,0:T(8,128)} fusion(bf16[4096,704]{1,0:T(8,128)(2,1)} %get-tuple-element.236, bf16[4096,2048]{1,0:T(8,128)(2,1)S(1)} %bitcast.159), kind=kOutput, calls=%fused_computation.172 | convolution fusion | flops 11811160064 | bytes 28311552 | tf_op jit(solution)/shard_map/dot_general | solution.py:995
  533.4 4.6 copy.100
  538.0 4.4 all-to-all-start.3
  547.7 2.7 bitcast_convert_fusion
  550.4 4.6 copy.83.gate_ref
  555.1 24.7 %collective-permute-done.36 = f32[15,2048]{1,0:T(8,128)S(1)} collective-permute-done((f32[15,2048]{1,0:T(8,128)S(1)}, f32[15,2048]{1,0:T(8,128)S(1)}, u32[]{:S(2)}, u32[]{:S(2)}) %collective-permute-start.36) | collective-permute-done | bytes 122912 | tf_op jit(solution)/shard_map/ppermute | solution.py:966
  580.1 3.0 collective-permute-done.38
  591.7 2.8 copy.84.wide_ref
  594.4 9.5 %place_w_gu.1 = f32[256,11264]{1,0:T(8,128)} custom-call(bf16[8,256,704]{2,1,0:T(8,128)(2,1)} %copy.83.gate_ref, bf16[8,256,704]{2,1,0:T(8,128)(2,1)} %copy.84.wide_ref), custom_call_target="tpu_custom_call" | custom-call | tf_op jit(solution)/shard_map/place_w_gu/pallas_call | solution.py:919
  604.0 31.6 %all-gather.13.cloned.1.call-done = bf16[32,64,1536]{2,1,0:T(8,128)(2,1)} async-done(((bf16[8,64,1536]{2,1,0:T(8,128)(2,1)}), bf16[32,64,1536]{2,1,0:T(8,128)(2,1)}) %all-gather.13.cloned.1.call-update) | async-done | bytes 6291472 | tf_op jit(solution)/shard_map/all_gather | solution.py:1250
  635.5 12.2 %place_w_in.1 = f32[256,12288]{1,0:T(8,128)} custom-call(bf16[4,8,64,1536]{3,2,1,0:T(8,128)(2,1)} %bitcast.175), custom_call_target="tpu_custom_call" | custom-call | tf_op jit(solution)/shard_map/place_w_in/pallas_call | solution.py:879
  (284 shorter events, 81.0 us)
Async XLA Ops:
  7.2 171.7 %all-gather.7.cloned.1.call-start = ((), (), s32[]{:S(2)}) async-start(), calls=%async_computation.5 | async-start | bytes 17301504 | tf_op jit(solution)/shard_map/all_gather | solution.py:1057
  13.3 28.4 %collective-permute-start.5 = (bf16[1024,3072]{1,0:T(8,128)(2,1)}, bf16[1024,3072]{1,0:T(8,128)(2,1)}, u32[]{:S(2)}, u32[]{:S(2)}) collective-permute-start(bf16[1024,3072]{1,0:T(8,128)(2,1)} %pick_heads.1.refs_4_), channel_id=1, source_target_pairs={{0,16},{16,0},{1,17},{17,1},{2,18},{18,2},{3,19},{19,3},{4,20},{20... | collective-permute-start | bytes 18874376 | tf_op jit(solution)/shard_map/ppermute | solution.py:966
  13.8 7.6 %collective-permute-start.1 = (bf16[128,2048]{1,0:T(8,128)(2,1)S(1)}, bf16[128,2048]{1,0:T(8,128)(2,1)S(1)}, u32[]{:S(2)}, u32[]{:S(2)}) collective-permute-start(bf16[128,2048]{1,0:T(8,128)(2,1)S(1)} %bitcast.184), channel_id=1, source_target_pairs={{0,16},{16,0},{1,17},{17,1},{2,18},{18,2},{3,19},{19,3},{4,20},{20... | collective-permute-start | bytes 1572872 | tf_op jit(solution)/shard_map/ppermute | solution.py:966
  13.9 16.5 %collective-permute-start.2 = (bf16[128,2048]{1,0:T(8,128)(2,1)S(1)}, bf16[128,2048]{1,0:T(8,128)(2,1)S(1)}, u32[]{:S(2)}, u32[]{:S(2)}) collective-permute-start(bf16[128,2048]{1,0:T(8,128)(2,1)S(1)} %bitcast.166), channel_id=1, source_target_pairs={{0,4},{4,0},{8,12},{12,8},{1,5},{5,1},{9,13},{13,9},{2,6},{6,2},{1... | collective-permute-start | bytes 1572872 | tf_op jit(solution)/shard_map/ppermute | solution.py:966
  16.9 24.9 %collective-permute-start.3 = (bf16[128,2048]{1,0:T(8,128)(2,1)S(1)}, bf16[128,2048]{1,0:T(8,128)(2,1)S(1)}, u32[]{:S(2)}, u32[]{:S(2)}) collective-permute-start(bf16[128,2048]{1,0:T(8,128)(2,1)S(1)} %bitcast.167), channel_id=1, source_target_pairs={{0,8},{4,12},{8,0},{12,4},{1,9},{5,13},{9,1},{13,5},{2,10},{6,14},... | collective-permute-start | bytes 1572872 | tf_op jit(solution)/shard_map/ppermute | solution.py:966
  18.4 23.4 %collective-permute-start.4 = (bf16[128,2048]{1,0:T(8,128)(2,1)S(1)}, bf16[128,2048]{1,0:T(8,128)(2,1)S(1)}, u32[]{:S(2)}, u32[]{:S(2)}) collective-permute-start(bf16[128,2048]{1,0:T(8,128)(2,1)S(1)} %bitcast.168), channel_id=1, source_target_pairs={{0,12},{4,8},{8,4},{12,0},{1,13},{5,9},{9,5},{13,1},{2,14},{6,10},... | collective-permute-start | bytes 1572872 | tf_op jit(solution)/shard_map/ppermute | solution.py:966
  41.8 172.9 %all-gather.9.cloned.1.call-start = ((), (), s32[]{:S(2)}) async-start(), calls=%async_computation.6 | async-start | bytes 2621440 | tf_op jit(solution)/shard_map/all_gather | solution.py:1086
  41.8 63.6 %collective-permute-start.11 = (bf16[1024,11264]{1,0:T(8,128)(2,1)}, bf16[1024,11264]{1,0:T(8,128)(2,1)}, u32[]{:S(2)}, u32[]{:S(2)}) collective-permute-start(bf16[1024,11264]{1,0:T(8,128)(2,1)} %refs_5_), channel_id=1, source_target_pairs={{0,16},{16,0},{1,17},{17,1},{2,18},{18,2},{3,19},{19,3},{4,20},{20... | collective-permute-start | bytes 69206024 | tf_op jit(solution)/shard_map/ppermute | solution.py:966
  41.9 63.5 %collective-permute-start.12 = (bf16[2048,2048]{1,0:T(8,128)(2,1)}, bf16[2048,2048]{1,0:T(8,128)(2,1)}, u32[]{:S(2)}, u32[]{:S(2)}) collective-permute-start(bf16[2048,2048]{1,0:T(8,128)(2,1)} %refs_2_), channel_id=1, source_target_pairs={{0,16},{16,0},{1,17},{17,1},{2,18},{18,2},{3,19},{19,3},{4,20},{20... | collective-permute-start | bytes 25165832 | tf_op jit(solution)/shard_map/ppermute | solution.py:966
  42.4 6.2 collective-permute-start
  42.5 22.0 %collective-permute-start.7 = (bf16[1024,32]{0,1:T(8,128)(2,1)S(1)}, bf16[1024,32]{0,1:T(8,128)(2,1)S(1)}, u32[]{:S(2)}, u32[]{:S(2)}) collective-permute-start(bf16[1024,32]{0,1:T(8,128)(2,1)S(1)} %copy-done.33), channel_id=1, source_target_pairs={{0,16},{16,0},{1,17},{17,1},{2,18},{18,2},{3,19},{19,3},{4,20},{20... | collective-permute-start | bytes 196616 | tf_op jit(solution)/shard_map/ppermute | solution.py:966
  42.9 6.3 collective-permute-start.6
  89.9 10.3 %collective-permute-start.10 = (bf16[128,1024]{1,0:T(8,128)(2,1)}, bf16[128,1024]{1,0:T(8,128)(2,1)S(1)}, u32[]{:S(2)}, u32[]{:S(2)}) collective-permute-start(bf16[128,1024]{1,0:T(8,128)(2,1)} %bitcast.220), channel_id=1, source_target_pairs={{0,12},{4,8},{8,4},{12,0},{1,13},{5,9},{9,5},{13,1},{2,14},{6,10},... | collective-permute-start | bytes 786440 | tf_op jit(solution)/shard_map/ppermute | solution.py:966
  91.5 13.9 %collective-permute-start.8 = (bf16[128,1024]{1,0:T(8,128)(2,1)}, bf16[128,1024]{1,0:T(8,128)(2,1)S(1)}, u32[]{:S(2)}, u32[]{:S(2)}) collective-permute-start(bf16[128,1024]{1,0:T(8,128)(2,1)} %bitcast.219), channel_id=1, source_target_pairs={{0,4},{4,0},{8,12},{12,8},{1,5},{5,1},{9,13},{13,9},{2,6},{6,2},{1... | collective-permute-start | bytes 786440 | tf_op jit(solution)/shard_map/ppermute | solution.py:966
  93.0 12.4 %collective-permute-start.9 = (bf16[128,1024]{1,0:T(8,128)(2,1)}, bf16[128,1024]{1,0:T(8,128)(2,1)S(1)}, u32[]{:S(2)}, u32[]{:S(2)}) collective-permute-start(bf16[128,1024]{1,0:T(8,128)(2,1)} %bitcast.218), channel_id=1, source_target_pairs={{0,8},{4,12},{8,0},{12,4},{1,9},{5,13},{9,1},{13,5},{2,10},{6,14},... | collective-permute-start | bytes 786440 | tf_op jit(solution)/shard_map/ppermute | solution.py:966
  117.4 3.6 collective-permute-start.13
  117.4 26.2 %collective-permute-start.14 = (bf16[128,1024]{1,0:T(8,128)(2,1)}, bf16[128,1024]{1,0:T(8,128)(2,1)S(1)}, u32[]{:S(2)}, u32[]{:S(2)}) collective-permute-start(bf16[128,1024]{1,0:T(8,128)(2,1)} %get-tuple-element.156), channel_id=1, source_target_pairs={{0,4},{4,0},{8,12},{12,8},{1,5},{5,1},{9,13},{13,9},{2,6},{6,2},{1... | collective-permute-start | bytes 786440 | tf_op jit(solution)/shard_map/ppermute | solution.py:966
  118.4 25.2 %collective-permute-start.15 = (bf16[128,1024]{1,0:T(8,128)(2,1)}, bf16[128,1024]{1,0:T(8,128)(2,1)S(1)}, u32[]{:S(2)}, u32[]{:S(2)}) collective-permute-start(bf16[128,1024]{1,0:T(8,128)(2,1)} %get-tuple-element.157), channel_id=1, source_target_pairs={{0,8},{4,12},{8,0},{12,4},{1,9},{5,13},{9,1},{13,5},{2,10},{6,14},... | collective-permute-start | bytes 786440 | tf_op jit(solution)/shard_map/ppermute | solution.py:966
  119.5 25.4 %collective-permute-start.16 = (bf16[128,1024]{1,0:T(8,128)(2,1)}, bf16[128,1024]{1,0:T(8,128)(2,1)S(1)}, u32[]{:S(2)}, u32[]{:S(2)}) collective-permute-start(bf16[128,1024]{1,0:T(8,128)(2,1)} %get-tuple-element.158), channel_id=1, source_target_pairs={{0,12},{4,8},{8,4},{12,0},{1,13},{5,9},{9,5},{13,1},{2,14},{6,10},... | collective-permute-start | bytes 786440 | tf_op jit(solution)/shard_map/ppermute | solution.py:966
  145.5 3.8 collective-permute-start.17
  163.7 13.0 %collective-permute-start.18 = (bf16[128,1024]{1,0:T(8,128)(2,1)}, bf16[128,1024]{1,0:T(8,128)(2,1)S(1)}, u32[]{:S(2)}, u32[]{:S(2)}) collective-permute-start(bf16[128,1024]{1,0:T(8,128)(2,1)} %get-tuple-element.163), channel_id=1, source_target_pairs={{0,4},{4,0},{8,12},{12,8},{1,5},{5,1},{9,13},{13,9},{2,6},{6,2},{1... | collective-permute-start | bytes 786440 | tf_op jit(solution)/shard_map/ppermute | solution.py:966
  163.8 12.9 %collective-permute-start.19 = (bf16[128,1024]{1,0:T(8,128)(2,1)}, bf16[128,1024]{1,0:T(8,128)(2,1)S(1)}, u32[]{:S(2)}, u32[]{:S(2)}) collective-permute-start(bf16[128,1024]{1,0:T(8,128)(2,1)} %get-tuple-element.164), channel_id=1, source_target_pairs={{0,8},{4,12},{8,0},{12,4},{1,9},{5,13},{9,1},{13,5},{2,10},{6,14},... | collective-permute-start | bytes 786440 | tf_op jit(solution)/shard_map/ppermute | solution.py:966
  164.8 14.2 %collective-permute-start.20 = (bf16[128,1024]{1,0:T(8,128)(2,1)}, bf16[128,1024]{1,0:T(8,128)(2,1)S(1)}, u32[]{:S(2)}, u32[]{:S(2)}) collective-permute-start(bf16[128,1024]{1,0:T(8,128)(2,1)} %get-tuple-element.165), channel_id=1, source_target_pairs={{0,12},{4,8},{8,4},{12,0},{1,13},{5,9},{9,5},{13,1},{2,14},{6,10},... | collective-permute-start | bytes 786440 | tf_op jit(solution)/shard_map/ppermute | solution.py:966
  179.6 23.8 %collective-permute-start.21 = (bf16[128,2048]{1,0:T(8,128)(2,1)S(1)}, bf16[128,2048]{1,0:T(8,128)(2,1)S(1)}, u32[]{:S(2)}, u32[]{:S(2)}) collective-permute-start(bf16[128,2048]{1,0:T(8,128)(2,1)S(1)} %copy-done.21), channel_id=1, source_target_pairs={{0,4},{4,0},{8,12},{12,8},{1,5},{5,1},{9,13},{13,9},{2,6},{6,2},{1... | collective-permute-start | bytes 1572872 | tf_op jit(solution)/shard_map/ppermute | solution.py:966
  181.1 24.6 %collective-permute-start.22 = (bf16[128,2048]{1,0:T(8,128)(2,1)S(1)}, bf16[128,2048]{1,0:T(8,128)(2,1)}, u32[]{:S(2)}, u32[]{:S(2)}) collective-permute-start(bf16[128,2048]{1,0:T(8,128)(2,1)S(1)} %copy-done.21), channel_id=1, source_target_pairs={{0,8},{4,12},{8,0},{12,4},{1,9},{5,13},{9,1},{13,5},{2,10},{6,14},... | collective-permute-start | bytes 1572872 | tf_op jit(solution)/shard_map/ppermute | solution.py:966
  182.0 23.6 %collective-permute-start.23 = (bf16[128,2048]{1,0:T(8,128)(2,1)S(1)}, bf16[128,2048]{1,0:T(8,128)(2,1)}, u32[]{:S(2)}, u32[]{:S(2)}) collective-permute-start(bf16[128,2048]{1,0:T(8,128)(2,1)S(1)} %copy-done.21), channel_id=1, source_target_pairs={{0,12},{4,8},{8,4},{12,0},{1,13},{5,9},{9,5},{13,1},{2,14},{6,10},... | collective-permute-start | bytes 1572872 | tf_op jit(solution)/shard_map/ppermute | solution.py:966
  183.1 37.6 %collective-permute-start.24 = (bf16[512,2048]{1,0:T(8,128)(2,1)S(1)}, bf16[512,2048]{1,0:T(8,128)(2,1)}, u32[]{:S(2)}, u32[]{:S(2)}) collective-permute-start(bf16[512,2048]{1,0:T(8,128)(2,1)S(1)} %copy-done.2), channel_id=1, source_target_pairs={{0,16},{16,0},{1,17},{17,1},{2,18},{18,2},{3,19},{19,3},{4,20},{20... | collective-permute-start | bytes 6291464 | tf_op jit(solution)/shard_map/ppermute | solution.py:966
  208.3 6.3 collective-permute-start.25
  233.5 98.3 %all-to-all-start = ((bf16[4,512,2048]{2,1,0:T(8,128)(2,1)}), bf16[4,512,2048]{2,1,0:T(8,128)(2,1)}, u32[]{:S(2)}, u32[]{:S(2)}) async-start(bf16[4,512,2048]{2,1,0:T(8,128)(2,1)} %broadcast_in_dim.8), calls=%async_computation.1 | async-start | bytes 16777216 | tf_op jit(solution)/shard_map/all_to_all | solution.py:1135
  239.2 210.9 %reduce-scatter.2.cloned.1.call-start = ((), (), s32[]{:S(2)}) async-start(), calls=%async_computation.7 | async-start | bytes 7864320 | tf_op jit(solution)/shard_map/reduce_scatter | solution.py:1134
  331.8 90.0 %collective-permute-start.34 = (bf16[2048,2048]{1,0:T(8,128)(2,1)}, bf16[2048,2048]{1,0:T(8,128)(2,1)}, u32[]{:S(2)}, u32[]{:S(2)}) collective-permute-start(bf16[2048,2048]{1,0:T(8,128)(2,1)} %bitcast.27.normed_ref), channel_id=1, source_target_pairs={{0,16},{16,0},{1,17},{17,1},{2,18},{18,2},{3,19},{19,3},{4,20},{20... | collective-permute-start | bytes 25165832 | tf_op jit(solution)/shard_map/ppermute | solution.py:966
  342.1 7.6 %collective-permute-start.29 = (bf16[512,2048]{1,0:T(8,128)(2,1)}, bf16[512,2048]{1,0:T(8,128)(2,1)}, u32[]{:S(2)}, u32[]{:S(2)}) collective-permute-start(bf16[512,2048]{1,0:T(8,128)(2,1)} %slice_bitcast_fusion), channel_id=1, source_target_pairs={{0,16},{16,0},{1,17},{17,1},{2,18},{18,2},{3,19},{19,3},{4,20},{20... | collective-permute-start | bytes 6291464 | tf_op jit(solution)/shard_map/ppermute | solution.py:966
  346.2 35.1 %collective-permute-start.26 = (bf16[128,2048]{1,0:T(8,128)(2,1)S(1)}, bf16[128,2048]{1,0:T(8,128)(2,1)S(1)}, u32[]{:S(2)}, u32[]{:S(2)}) collective-permute-start(bf16[128,2048]{1,0:T(8,128)(2,1)S(1)} %get-tuple-element.257), channel_id=1, source_target_pairs={{0,4},{4,0},{8,12},{12,8},{1,5},{5,1},{9,13},{13,9},{2,6},{6,2},{1... | collective-permute-start | bytes 1572872 | tf_op jit(solution)/shard_map/ppermute | solution.py:966
  347.7 35.4 %collective-permute-start.27 = (bf16[128,2048]{1,0:T(8,128)(2,1)S(1)}, bf16[128,2048]{1,0:T(8,128)(2,1)}, u32[]{:S(2)}, u32[]{:S(2)}) collective-permute-start(bf16[128,2048]{1,0:T(8,128)(2,1)S(1)} %get-tuple-element.259), channel_id=1, source_target_pairs={{0,8},{4,12},{8,0},{12,4},{1,9},{5,13},{9,1},{13,5},{2,10},{6,14},... | collective-permute-start | bytes 1572872 | tf_op jit(solution)/shard_map/ppermute | solution.py:966
  348.2 37.4 %collective-permute-start.28 = (bf16[128,2048]{1,0:T(8,128)(2,1)S(1)}, bf16[128,2048]{1,0:T(8,128)(2,1)}, u32[]{:S(2)}, u32[]{:S(2)}) collective-permute-start(bf16[128,2048]{1,0:T(8,128)(2,1)S(1)} %get-tuple-element.258), channel_id=1, source_target_pairs={{0,12},{4,8},{8,4},{12,0},{1,13},{5,9},{9,5},{13,1},{2,14},{6,10},... | collective-permute-start | bytes 1572872 | tf_op jit(solution)/shard_map/ppermute | solution.py:966
  353.1 35.6 %collective-permute-start.30 = (bf16[128,2048]{1,0:T(8,128)(2,1)}, bf16[128,2048]{1,0:T(8,128)(2,1)S(1)}, u32[]{:S(2)}, u32[]{:S(2)}) collective-permute-start(bf16[128,2048]{1,0:T(8,128)(2,1)} %get-tuple-element.255), channel_id=1, source_target_pairs={{0,1},{1,0},{2,3},{3,2},{4,5},{5,4},{6,7},{7,6},{8,9},{9,8},{10,11... | collective-permute-start | bytes 1572872 | tf_op jit(solution)/shard_map/ppermute | solution.py:966
  381.3 37.8 %collective-permute-start.31 = (bf16[128,2048]{1,0:T(8,128)(2,1)}, bf16[128,2048]{1,0:T(8,128)(2,1)S(1)}, u32[]{:S(2)}, u32[]{:S(2)}) collective-permute-start(bf16[128,2048]{1,0:T(8,128)(2,1)} %get-tuple-element.254), channel_id=1, source_target_pairs={{0,2},{1,3},{2,0},{3,1},{4,6},{5,7},{6,4},{7,5},{8,10},{9,11},{10,... | collective-permute-start | bytes 1572872 | tf_op jit(solution)/shard_map/ppermute | solution.py:966
  383.1 36.0 %collective-permute-start.32 = (bf16[128,2048]{1,0:T(8,128)(2,1)}, bf16[128,2048]{1,0:T(8,128)(2,1)S(1)}, u32[]{:S(2)}, u32[]{:S(2)}) collective-permute-start(bf16[128,2048]{1,0:T(8,128)(2,1)} %get-tuple-element.253), channel_id=1, source_target_pairs={{0,3},{1,2},{2,1},{3,0},{4,7},{5,6},{6,5},{7,4},{8,11},{9,10},{10,... | collective-permute-start | bytes 1572872 | tf_op jit(solution)/shard_map/ppermute | solution.py:966
  419.3 1.4 collective-permute-start.33
  450.1 32.8 %all-to-all-start.1 = ((bf16[8,64,1536]{2,1,0:T(8,128)(2,1)}), bf16[8,64,1536]{2,1,0:T(8,128)(2,1)S(1)}, u32[]{:S(2)}, u32[]{:S(2)}) async-start(bf16[8,64,1536]{2,1,0:T(8,128)(2,1)} %bitcast.186), calls=%async_computation.2 | async-start | bytes 3145728 | tf_op jit(solution)/shard_map/all_to_all | solution.py:1182
  453.8 79.6 %all-gather.11.cloned.1.call-start = ((), (), s32[]{:S(2)}) async-start(), calls=%async_computation.8 | async-start | bytes 3276800 | tf_op jit(solution)/shard_map/all_gather | solution.py:1240
  454.4 181.1 %all-gather.13.cloned.1.call-start = ((), (), s32[]{:S(2)}) async-start(), calls=%async_computation.9 | async-start | bytes 7864320 | tf_op jit(solution)/shard_map/all_gather | solution.py:1250
  463.1 21.1 %collective-permute-start.35 = (f32[128,2048]{1,0:T(8,128)}, f32[128,2048]{1,0:T(8,128)}, u32[]{:S(2)}, u32[]{:S(2)}) collective-permute-start(f32[128,2048]{1,0:T(8,128)} %slice.168), channel_id=1, source_target_pairs={{0,16},{16,0},{1,17},{17,1},{2,18},{18,2},{3,19},{19,3},{4,20},{20... | collective-permute-start | bytes 3145736 | tf_op jit(solution)/shard_map/ppermute | solution.py:966
  488.7 44.7 %all-to-all-start.2 = ((bf16[8,256,704]{1,2,0:T(8,128)(2,1)}), bf16[8,256,704]{1,2,0:T(8,128)(2,1)S(1)}, u32[]{:S(2)}, u32[]{:S(2)}) async-start(bf16[8,256,704]{1,2,0:T(8,128)(2,1)} %bitcast.170), calls=%async_computation.3 | async-start | bytes 5767168 | tf_op jit(solution)/shard_map/all_to_all | solution.py:1182
  538.0 53.7 %all-to-all-start.3 = ((bf16[8,256,704]{1,2,0:T(8,128)(2,1)}), bf16[8,256,704]{1,2,0:T(8,128)(2,1)S(1)}, u32[]{:S(2)}, u32[]{:S(2)}) async-start(bf16[8,256,704]{1,2,0:T(8,128)(2,1)} %bitcast.169), calls=%async_computation.4 | async-start | bytes 5767168 | tf_op jit(solution)/shard_map/all_to_all | solution.py:1182
  543.8 36.0 %collective-permute-start.36 = (f32[15,2048]{1,0:T(8,128)S(1)}, f32[15,2048]{1,0:T(8,128)S(1)}, u32[]{:S(2)}, u32[]{:S(2)}) collective-permute-start(f32[15,2048]{1,0:T(8,128)S(1)} %fusion.17), channel_id=1, source_target_pairs={{0,4},{4,0},{8,12},{12,8},{1,5},{5,1},{9,13},{13,9},{2,6},{6,2},{1... | collective-permute-start | bytes 368648 | tf_op jit(solution)/shard_map/ppermute | solution.py:966
  545.9 34.0 %collective-permute-start.37 = (f32[15,2048]{1,0:T(8,128)S(1)}, f32[15,2048]{1,0:T(8,128)S(1)}, u32[]{:S(2)}, u32[]{:S(2)}) collective-permute-start(f32[15,2048]{1,0:T(8,128)S(1)} %fusion.17), channel_id=1, source_target_pairs={{0,8},{4,12},{8,0},{12,4},{1,9},{5,13},{9,1},{13,5},{2,10},{6,14},... | collective-permute-start | bytes 368648 | tf_op jit(solution)/shard_map/ppermute | solution.py:966
  547.4 35.7 %collective-permute-start.38 = (f32[15,2048]{1,0:T(8,128)S(1)}, f32[15,2048]{1,0:T(8,128)S(1)}, u32[]{:S(2)}, u32[]{:S(2)}) collective-permute-start(f32[15,2048]{1,0:T(8,128)S(1)} %fusion.17), channel_id=1, source_target_pairs={{0,12},{4,8},{8,4},{12,0},{1,13},{5,9},{9,5},{13,1},{2,14},{6,10},... | collective-permute-start | bytes 368648 | tf_op jit(solution)/shard_map/ppermute | solution.py:966
  (50 other events, 539.3 us)
Sparse Core Ops, SparseCore 0:
  41.9 126.4 all-gather.6
  170.5 44.0 all-gather.8
  242.3 109.9 reduce-scatter.1
  455.9 63.9 all-gather.10
  521.4 114.1 all-gather.12
where the time goes:
time: 662 us; the launch traced here: 655 us
  waiting for transfers between devices  211 us (32%)
  Pallas kernels  206 us (31%)
  matrix products  92.2 us (14%)
  local copies, waits for them, and re-layouts  57.3 us (9%)
  starting transfers between devices  51 us (8%)
  other arithmetic  22.1 us (3%)
  between operations  14.9 us (2%)
    ppermute x39, waiting for transfers between devices, swapped(): lax.ppermute(value, axis, [(source, source ^ step) for source in range(co...  95.8 us
    all_to_all x1, waiting for transfers between devices, body(): lax.all_to_all(spread, 'seq', split_axis=0, concat_axis=0).reshape(-1, D)  75.9 us
    dot_general x5, matrix products, dot_cols(): lax.dot_general(left, right, (((0,), (0,)), ((), ())), preferred_element_...  59.7 us
    pallas_call x2, Pallas kernels, feed_again(): pl.pallas_call(functools.partial(again_kernel, parts), grid_spec=pltpu.Pr...  56.4 us
    ppermute x39, starting transfers between devices, swapped(): lax.ppermute(value, axis, [(source, source ^ step) for source in range(co...  32.8 us
    all_gather x1, waiting for transfers between devices, body(): grad_in = lax.all_gather(grad_in, 'replica', axis=0)  31.6 us
    pallas_call x1, Pallas kernels, mixer_forward(): pl.pallas_call(forward_kernel, grid_spec=pltpu.PrefetchScalarGridSpec(num...  22.4 us
    pallas_call x1, Pallas kernels, feed(): pl.pallas_call(functools.partial(feed_kernel, parts), grid_spec=pltpu.Pre...  21.9 us
  transfers between devices with their start and end apart: 48, of which 15 were waited for; matrix products, arithmetic and copies ran while one was open for 25% of the time, Pallas kernels for 27%

commit v1 on v0

--- a/solution.py
+++ b/solution.py
@@ -1185,6 +1185,7 @@
         return to_group(value.astype(BF16).reshape(owners, D // owners, ff_own))
 
     normed_parts = input_gradient_parts(proj_grad, small_grad)
+    own_renormed, grad_out, *normed_parts = pinned(own_renormed, grad_out, *normed_parts)
     replica = lax.axis_index("replica")
     grad_out = [
         swapped(part_of(grad_out, jnp.bitwise_xor(replica, step), replicas, 0), "replica", step)
@@ -1192,7 +1193,6 @@
         else part_of(grad_out, replica, replicas, 0)
         for step in range(replicas)
     ]
-    own_renormed, *normed_parts = pinned(own_renormed, *normed_parts)
     input_grads, gain1_grad, grad_ab, params_grad = input_gradient(*normed_parts)
     gain2_grad = gain2_grad[0]
     all_renormed = around(own_renormed, "shard")

time: 662 us -> 653 us (0.986)
  waiting for transfers between devices: 211 us -> 199 us
    all_to_all x1, waiting for transfers between devices: 75.9 us -> 64.7 us  [body(): lax.all_to_all(spread, 'seq', split_axis=0, concat_axis=0).reshape(-1, D)]
  transfers between devices with their start and end apart: 48 -> 48, of which waited for: 15 -> 14; matrix products, arithmetic and copies ran while one was open for 25% -> 26% of each run, Pallas kernels for 27% -> 27%
where the time goes in v1:
time: 653 us; the launch traced here: 645 us
  Pallas kernels  206 us (32%)
  waiting for transfers between devices  199 us (30%)
  matrix products  94.4 us (14%)
  local copies, waits for them, and re-layouts  57 us (9%)
  starting transfers between devices  50.4 us (8%)
  other arithmetic  22.9 us (4%)
  between operations  14.9 us (2%)
    ppermute x39, waiting for transfers between devices, swapped(): lax.ppermute(value, axis, [(source, source ^ step) for source in range(co...  95.2 us
    all_to_all x1, waiting for transfers between devices, body(): lax.all_to_all(spread, 'seq', split_axis=0, concat_axis=0).reshape(-1, D)  64.7 us
    dot_general x5, matrix products, dot_cols(): lax.dot_general(left, right, (((0,), (0,)), ((), ())), preferred_element_...  59.6 us
    pallas_call x2, Pallas kernels, feed_again(): pl.pallas_call(functools.partial(again_kernel, parts), grid_spec=pltpu.Pr...  56.5 us
    ppermute x39, starting transfers between devices, swapped(): lax.ppermute(value, axis, [(source, source ^ step) for source in range(co...  32.3 us
    all_gather x1, waiting for transfers between devices, body(): grad_in = lax.all_gather(grad_in, 'replica', axis=0)  31.6 us
    pallas_call x1, Pallas kernels, mixer_forward(): pl.pallas_call(forward_kernel, grid_spec=pltpu.PrefetchScalarGridSpec(num...  22.5 us
    pallas_call x1, Pallas kernels, feed(): pl.pallas_call(functools.partial(feed_kernel, parts), grid_spec=pltpu.Pre...  21.8 us
  transfers between devices with their start and end apart: 48, of which 14 were waited for; matrix products, arithmetic and copies ran while one was open for 26% of the time, Pallas kernels for 27%

profile of v1, /device:TPU:0, one launch (start us, length us, event | category | flops | bytes accessed | tf_op | source)
XLA Modules:
  0.0 644.5 jit_solution(10971773888432821357)
XLA Ops:
  7.3 6.1 pick_heads.1.refs_4_
  13.9 2.9 collective-permute-start.2
  18.4 3.0 collective-permute-done.1
  21.4 9.0 %fusion.10.refs_2_ = f32[256,2816]{1,0:T(8,128)} fusion(bf16[2816,2048]{1,0:T(8,128)(2,1)} %param.23, bf16[128,2048]{1,0:T(8,128)(2,1)S(1)} %collective-permute-done.1, bf16[128,2048]{1,0:T(8,128)(2,1)S(1)} %bitcast.185), kind=kOutput, calls=%fused_computation.29 | convolution fusion | flops 2954887168 | bytes 15466496 | tf_op jit(solution)/shard_map/dot_general | solution.py:991
  30.5 11.3 %collective-permute-done.3.refs_2_ = bf16[128,2048]{1,0:T(8,128)(2,1)S(1)} collective-permute-done((bf16[128,2048]{1,0:T(8,128)(2,1)S(1)}, bf16[128,2048]{1,0:T(8,128)(2,1)S(1)}, u32[]{:S(2)}, u32[]{:S(2)}) %collective-permute-start.3) | collective-permute-done | bytes 524320 | tf_op jit(solution)/shard_map/ppermute | solution.py:966
  43.2 5.4 collective-permute-done
  50.0 12.9 %project.1 = (bf16[512,2048]{1,0:T(8,128)(2,1)}, f32[512,3072]{1,0:T(8,128)}) custom-call(s32[1]{0:T(128)} %bitcast.1.place_ref, f32[1,2048]{1,0:T(1,128)} %get-tuple-element.284.gain_ref, bf16[128,2048]{1,0:T(8,128)(2,1)} %bitcast.164, bf16[128,2048]{1,0:T(8,128)(2,1)} %copy-done.18, bf16[128,2048]{1,0:T(8,128)(2,1)} %copy-done.19, ...), custom_call_target="tpu_custom_call" | custom-call | tf_op jit(solution)/shard_map/project/pallas_call | solution.py:433
  67.5 22.5 %mixer_forward.1 = (bf16[2,64,1024]{2,1,0:T(8,128)(2,1)}, bf16[2,64,1024]{2,1,0:T(8,128)(2,1)}, bf16[2,64,1024]{2,1,0:T(8,128)(2,1)}, bf16[2,64,1024]{2,1,0:T(8,...) custom-call(s32[1]{0:T(128)} %bitcast.place_ref, f32[4,2,64,3072]{3,2,1,0:T(8,128)} %bitcast.162, ...), custom_call_target="tpu_custom_call" | custom-call | tf_op jit(solution)/shard_map/mixer_forward/pallas_call | solution.py:323
  94.1 6.2 collective-permute-done.10.refs_3_
  100.3 5.1 collective-permute-done.8.refs_1_
  106.2 11.1 %merge_heads.1 = (f32[128,2048]{1,0:T(8,128)}, bf16[128,2048]{1,0:T(8,128)(2,1)}, bf16[128,1024]{1,0:T(8,128)(2,1)}, bf16[128,1024]{1,0:T(8,128)(2,1)}, bf16[128...) custom-call(s32[2]{0:T(128)} %pad_add_fusion.places_ref, f32[1,2048]{1,0:T(1,128)} %get-tuple-element.283.gain_ref, ...), custom_call_target="tpu_custom_call" | custom-call | tf_op jit(solution)/shard_map/merge_heads/pallas_call | solution.py:509
  121.6 21.8 %feed_forward.1 = (f32[2,128,1024]{2,1,0:T(8,128)}, f32[2,128,1024]{2,1,0:T(8,128)}, bf16[256,2816]{1,0:T(8,128)(2,1)}) custom-call(s32[2]{0:T(128)} %pad_add_fusion.places_ref, bf16[128,2048]{1,0:T(8,128)(2,1)} %get-tuple-element.149.refs_0_, bf16[128,2048]{1,0:T(8,128)(2,1)} %copy-done.17, f32[256,2816]{1,0:T(8,128)} %fusion.10.refs_2_, ...), custom_call_target="tpu_custom_call" | custom-call | tf_op jit(solution)/shard_map/feed_forward/pallas_call | solution.py:601
  145.6 3.8 constant_dynamic-slice_fusion.19.refs_4_
  150.3 13.4 %split_heads.1 = (f32[128,2048]{1,0:T(8,128)}, bf16[128,2048]{1,0:T(8,128)(2,1)}, f32[1,2048]{1,0:T(1,128)}, bf16[128,1024]{1,0:T(8,128)(2,1)}, bf16[128,1024]{1...) custom-call(s32[2]{0:T(128)} %pad_add_fusion.places_ref, f32[1,2048]{1,0:T(1,128)} %get-tuple-element.283.gain_ref, ...), custom_call_target="tpu_custom_call" | custom-call | tf_op jit(solution)/shard_map/split_heads/pallas_call | solution.py:679
  167.2 9.5 %constant_dynamic-slice_fusion.15 = (bf16[1024,704]{1,0:T(8,128)(2,1)}, bf16[1024,704]{1,0:T(8,128)(2,1)}, bf16[1024,704]{1,0:T(8,128)(2,1)}, bf16[1024,704]{1,0:T(8,128)(2,1)}) fusion(bf16[1024,11264]{1,0:T(8,128)(2,1)} %collective-permute-done.11.refs_4_.refs_6_, s32[]{:T(128)S(6)} %select_n.120, s32[]{:T(128)S(6)} %select_n.119, bf16[1024,11264]{1,0:T(8,128)(2,1)} %refs_5_), kind=kLoop, calls=%fused_computation.107 | loop fusion | bytes 11534344 | tf_op jit(solution)/shard_map/dynamic_slice | solution.py:983
  183.0 20.3 %mixer_backward.1 = (bf16[4,2,64,3072]{3,2,1,0:T(8,128)(2,1)}, f32[2,4,8,512]{3,2,1,0:T(8,128)}) custom-call(s32[1]{0:T(128)} %bitcast.place_ref, f32[4,2,64,3072]{3,2,1,0:T(8,128)} %bitcast.163, bf16[4,8192]{1,0:T(4,128)(2,1)} %pad_maximum_fusion.3.taps_q.taps_k.taps_v, bf16[4,8192]{1,0:T(4,128)(2,1)} %pad_maximum_fusion.3.taps_q.taps_k.taps_v, ...), custom_call_target="tpu_custom_call" | custom-call | tf_op jit(solution)/shard_map/mixer_backward/pallas_call | solution.py:349
  205.7 2.7 constant_dynamic-slice_fusion.14
  208.3 6.4 all-gather.9.cloned.1.call-done
  214.7 6.1 broadcast_in_dim.8
  220.8 12.8 %outer_products.1 = bf16[4,8,64,1536]{3,2,1,0:T(8,128)(2,1)} custom-call(s32[2]{0:T(128)} %pad_add_fusion.places_ref, bf16[512,2048]{1,0:T(8,128)(2,1)} %get-tuple-element.134.refs_0_, bf16[512,2048]{1,0:T(8,128)(2,1)} %collective-permute-done.24.refs_1_, bf16[512,3072]{1,0:T(8,128)(2,1)} %bitcast.172, bf16[512,1536]{1,0:T(8,128)(2,1)} %collective-permute-done.25.refs_3_), custom_call_target="tpu_custom_call" | custom-call | tf_op jit(solution)/shard_map/outer_products/pallas_call | solution.py:723
  233.6 5.8 all-to-all-start
  241.0 7.2 %own_rows.1 = bf16[2,512,2048]{2,1,0:T(8,128)(2,1)} custom-call(s32[2]{0:T(128)} %pad_add_fusion.places_ref, bf16[128,1024]{1,0:T(8,128)(2,1)} %get-tuple-element.184.refs_0_, bf16[128,1024]{1,0:T(8,128)(2,1)} %copy-done.29, bf16[128,1024]{1,0:T(8,128)(2,1)} %copy-done.30, bf16[128,1024]{1,0:T(8,128)(2,1)} %copy-done.31, ...), custom_call_target="tpu_custom_call" | custom-call | tf_op jit(solution)/shard_map/own_rows/pallas_call | solution.py:768
  253.7 7.9 %convolution_add_fusion = f32[512,1024]{1,0:T(8,128)} fusion(f32[512,1024]{1,0:T(8,128)S(1)} %fusion.54, bf16[512,3072]{1,0:T(8,128)(2,1)S(1)} %bitcast.173, bf16[1024,3072]{1,0:T(8,128)(2,1)} %collective-permute-done.5.refs_5_), kind=kOutput, calls=%fused_computation.21 | convolution fusion | flops 3221749760 | bytes 13631488 | tf_op jit(solution)/shard_map/dot_general | solution.py:991
  261.6 4.8 convolution_add_fusion.1
  267.2 64.7 %all-to-all-done = bf16[4,512,2048]{2,1,0:T(8,128)(2,1)} async-done(((bf16[4,512,2048]{2,1,0:T(8,128)(2,1)}), bf16[4,512,2048]{2,1,0:T(8,128)(2,1)}, u32[]{:S(2)}, u32[]{:S(2)}) %all-to-all-start) | async-done | bytes 8388640 | tf_op jit(solution)/shard_map/all_to_all | solution.py:1135
  332.4 3.7 fusion.5
  342.2 28.5 %feed_again.2 = (bf16[4096,704]{1,0:T(8,128)(2,1)}, bf16[2048,704]{1,0:T(8,128)(2,1)}, bf16[2048,704]{1,0:T(8,128)(2,1)}) custom-call(s32[2]{0:T(128)} %pad_add_fusion.places_ref, bf16[2048,2048]{1,0:T(8,128)(2,1)} %bitcast.27.normed_ref, bf16[4096,2048]{1,0:T(8,128)(2,1)} %all-gather.7.cloned.1.call-done.up_ref, ...), custom_call_target="tpu_custom_call" | custom-call | tf_op jit(solution)/shard_map/feed_again/pallas_call | solution.py:814
  378.3 30.8 %collective-permute-done.31 = bf16[128,2048]{1,0:T(8,128)(2,1)S(1)} collective-permute-done((bf16[128,2048]{1,0:T(8,128)(2,1)}, bf16[128,2048]{1,0:T(8,128)(2,1)S(1)}, u32[]{:S(2)}, u32[]{:S(2)}) %collective-permute-start.31) | collective-permute-done | bytes 524320 | tf_op jit(solution)/shard_map/ppermute | solution.py:966
  411.7 28.1 %feed_again.3 = (bf16[4096,704]{1,0:T(8,128)(2,1)}, bf16[2048,704]{1,0:T(8,128)(2,1)}, bf16[2048,704]{1,0:T(8,128)(2,1)}) custom-call(s32[2]{0:T(128)} %pad_add_fusion.places_ref, bf16[2048,2048]{1,0:T(8,128)(2,1)} %collective-permute-done.34.normed_ref, bf16[4096,2048]{1,0:T(8,128)(2,1)} %all-gather.7.cloned.1.call-done.up_ref, ...), custom_call_target="tpu_custom_call", output_to_operand_aliasing={{0}: (8, {})} | custom-call | tf_op jit(solution)/shard_map/feed_again/pallas_call | solution.py:814
  439.8 3.7 all-to-all-start.1
  444.2 6.7 %fusion.56 = f32[256,2048]{1,0:T(8,128)S(1)} fusion(bf16[256,2816]{1,0:T(8,128)(2,1)S(1)} %copy-done.43, bf16[2816,2048]{1,0:T(8,128)(2,1)} %param.23), kind=kOutput, calls=%fused_computation.169 | convolution fusion | flops 2952790016 | bytes 15073280 | tf_op jit(solution)/shard_map/dot_general | solution.py:987
  453.8 9.0 %fusion.57 = f32[2048,704]{0,1:T(8,128)S(1)} fusion(bf16[2048,2048]{1,0:T(8,128)(2,1)} %collective-permute-done.34.normed_ref, bf16[2048,704]{1,0:T(8,128)(2,1)S(1)} %copy-done.42), kind=kOutput, calls=%fused_computation.170 | convolution fusion | flops 5905580032 | bytes 17039360 | tf_op jit(solution)/shard_map/dot_general | solution.py:995
  462.8 10.3 %add_convert_fusion.1 = bf16[2048,704]{0,1:T(8,128)(2,1)} fusion(f32[2048,704]{0,1:T(8,128)S(1)} %fusion.57, bf16[2048,2048]{1,0:T(8,128)(2,1)} %bitcast.27.normed_ref, bf16[2048,704]{1,0:T(8,128)(2,1)S(1)} %copy-done.41), kind=kOutput, calls=%fused_computation.1 | convolution fusion | flops 5908463616 | bytes 19922944 | tf_op jit(solution)/shard_map/dot_general | solution.py:995
  474.4 2.8 fusion.9
  478.9 4.0 all-to-all-start.2
  483.0 11.3 %fusion.58 = f32[2048,704]{0,1:T(8,128)} fusion(bf16[2048,2048]{1,0:T(8,128)(2,1)} %collective-permute-done.34.normed_ref, bf16[2048,704]{1,0:T(8,128)(2,1)} %get-tuple-element.231), kind=kOutput, calls=%fused_computation.171 | convolution fusion | flops 5905580032 | bytes 17039360 | tf_op jit(solution)/shard_map/dot_general | solution.py:995
  494.3 12.3 %add_convert_fusion = bf16[2048,704]{0,1:T(8,128)(2,1)} fusion(f32[2048,704]{0,1:T(8,128)} %fusion.58, bf16[2048,2048]{1,0:T(8,128)(2,1)} %bitcast.27.normed_ref, bf16[2048,704]{1,0:T(8,128)(2,1)S(1)} %copy-done.40), kind=kOutput, calls=%fused_computation | convolution fusion | flops 5908463616 | bytes 19922944 | tf_op jit(solution)/shard_map/dot_general | solution.py:995
  506.6 16.7 %fusion.59 = f32[704,2048]{1,0:T(8,128)} fusion(bf16[4096,704]{1,0:T(8,128)(2,1)} %get-tuple-element.238, bf16[4096,2048]{1,0:T(8,128)(2,1)S(1)} %bitcast.159), kind=kOutput, calls=%fused_computation.172 | convolution fusion | flops 11811160064 | bytes 28311552 | tf_op jit(solution)/shard_map/dot_general | solution.py:995
  523.4 4.6 copy.100
  528.0 4.4 all-to-all-start.3
  537.7 2.7 bitcast_convert_fusion
  540.4 4.6 copy.83.gate_ref
  545.1 24.7 %collective-permute-done.36 = f32[15,2048]{1,0:T(8,128)S(1)} collective-permute-done((f32[15,2048]{1,0:T(8,128)S(1)}, f32[15,2048]{1,0:T(8,128)S(1)}, u32[]{:S(2)}, u32[]{:S(2)}) %collective-permute-start.36) | collective-permute-done | bytes 122912 | tf_op jit(solution)/shard_map/ppermute | solution.py:966
  570.1 3.0 collective-permute-done.38
  581.6 2.8 copy.84.wide_ref
  584.4 9.5 %place_w_gu.1 = f32[256,11264]{1,0:T(8,128)} custom-call(bf16[8,256,704]{2,1,0:T(8,128)(2,1)} %copy.83.gate_ref, bf16[8,256,704]{2,1,0:T(8,128)(2,1)} %copy.84.wide_ref), custom_call_target="tpu_custom_call" | custom-call | tf_op jit(solution)/shard_map/place_w_gu/pallas_call | solution.py:919
  593.9 31.6 %all-gather.13.cloned.1.call-done = bf16[32,64,1536]{2,1,0:T(8,128)(2,1)} async-done(((bf16[8,64,1536]{2,1,0:T(8,128)(2,1)}), bf16[32,64,1536]{2,1,0:T(8,128)(2,1)}) %all-gather.13.cloned.1.call-update) | async-done | bytes 6291472 | tf_op jit(solution)/shard_map/all_gather | solution.py:1250
  625.5 12.2 %place_w_in.1 = f32[256,12288]{1,0:T(8,128)} custom-call(bf16[4,8,64,1536]{3,2,1,0:T(8,128)(2,1)} %bitcast.175), custom_call_target="tpu_custom_call" | custom-call | tf_op jit(solution)/shard_map/place_w_in/pallas_call | solution.py:879
  (284 shorter events, 79.1 us)
Async XLA Ops:
  7.2 171.6 %all-gather.7.cloned.1.call-start = ((), (), s32[]{:S(2)}) async-start(), calls=%async_computation.5 | async-start | bytes 17301504 | tf_op jit(solution)/shard_map/all_gather | solution.py:1057
  13.3 28.4 %collective-permute-start.5 = (bf16[1024,3072]{1,0:T(8,128)(2,1)}, bf16[1024,3072]{1,0:T(8,128)(2,1)}, u32[]{:S(2)}, u32[]{:S(2)}) collective-permute-start(bf16[1024,3072]{1,0:T(8,128)(2,1)} %pick_heads.1.refs_4_), channel_id=1, source_target_pairs={{0,16},{16,0},{1,17},{17,1},{2,18},{18,2},{3,19},{19,3},{4,20},{20... | collective-permute-start | bytes 18874376 | tf_op jit(solution)/shard_map/ppermute | solution.py:966
  13.8 7.6 %collective-permute-start.1 = (bf16[128,2048]{1,0:T(8,128)(2,1)S(1)}, bf16[128,2048]{1,0:T(8,128)(2,1)S(1)}, u32[]{:S(2)}, u32[]{:S(2)}) collective-permute-start(bf16[128,2048]{1,0:T(8,128)(2,1)S(1)} %bitcast.184), channel_id=1, source_target_pairs={{0,16},{16,0},{1,17},{17,1},{2,18},{18,2},{3,19},{19,3},{4,20},{20... | collective-permute-start | bytes 1572872 | tf_op jit(solution)/shard_map/ppermute | solution.py:966
  13.9 16.5 %collective-permute-start.2 = (bf16[128,2048]{1,0:T(8,128)(2,1)S(1)}, bf16[128,2048]{1,0:T(8,128)(2,1)S(1)}, u32[]{:S(2)}, u32[]{:S(2)}) collective-permute-start(bf16[128,2048]{1,0:T(8,128)(2,1)S(1)} %bitcast.166), channel_id=1, source_target_pairs={{0,4},{4,0},{8,12},{12,8},{1,5},{5,1},{9,13},{13,9},{2,6},{6,2},{1... | collective-permute-start | bytes 1572872 | tf_op jit(solution)/shard_map/ppermute | solution.py:966
  16.9 24.9 %collective-permute-start.3 = (bf16[128,2048]{1,0:T(8,128)(2,1)S(1)}, bf16[128,2048]{1,0:T(8,128)(2,1)S(1)}, u32[]{:S(2)}, u32[]{:S(2)}) collective-permute-start(bf16[128,2048]{1,0:T(8,128)(2,1)S(1)} %bitcast.167), channel_id=1, source_target_pairs={{0,8},{4,12},{8,0},{12,4},{1,9},{5,13},{9,1},{13,5},{2,10},{6,14},... | collective-permute-start | bytes 1572872 | tf_op jit(solution)/shard_map/ppermute | solution.py:966
  18.4 23.4 %collective-permute-start.4 = (bf16[128,2048]{1,0:T(8,128)(2,1)S(1)}, bf16[128,2048]{1,0:T(8,128)(2,1)S(1)}, u32[]{:S(2)}, u32[]{:S(2)}) collective-permute-start(bf16[128,2048]{1,0:T(8,128)(2,1)S(1)} %bitcast.168), channel_id=1, source_target_pairs={{0,12},{4,8},{8,4},{12,0},{1,13},{5,9},{9,5},{13,1},{2,14},{6,10},... | collective-permute-start | bytes 1572872 | tf_op jit(solution)/shard_map/ppermute | solution.py:966
  41.8 172.9 %all-gather.9.cloned.1.call-start = ((), (), s32[]{:S(2)}) async-start(), calls=%async_computation.6 | async-start | bytes 2621440 | tf_op jit(solution)/shard_map/all_gather | solution.py:1086
  41.8 63.6 %collective-permute-start.11 = (bf16[1024,11264]{1,0:T(8,128)(2,1)}, bf16[1024,11264]{1,0:T(8,128)(2,1)}, u32[]{:S(2)}, u32[]{:S(2)}) collective-permute-start(bf16[1024,11264]{1,0:T(8,128)(2,1)} %refs_5_), channel_id=1, source_target_pairs={{0,16},{16,0},{1,17},{17,1},{2,18},{18,2},{3,19},{19,3},{4,20},{20... | collective-permute-start | bytes 69206024 | tf_op jit(solution)/shard_map/ppermute | solution.py:966
  41.9 63.5 %collective-permute-start.12 = (bf16[2048,2048]{1,0:T(8,128)(2,1)}, bf16[2048,2048]{1,0:T(8,128)(2,1)}, u32[]{:S(2)}, u32[]{:S(2)}) collective-permute-start(bf16[2048,2048]{1,0:T(8,128)(2,1)} %refs_2_), channel_id=1, source_target_pairs={{0,16},{16,0},{1,17},{17,1},{2,18},{18,2},{3,19},{19,3},{4,20},{20... | collective-permute-start | bytes 25165832 | tf_op jit(solution)/shard_map/ppermute | solution.py:966
  42.4 6.2 collective-permute-start
  42.5 22.0 %collective-permute-start.7 = (bf16[1024,32]{0,1:T(8,128)(2,1)S(1)}, bf16[1024,32]{0,1:T(8,128)(2,1)S(1)}, u32[]{:S(2)}, u32[]{:S(2)}) collective-permute-start(bf16[1024,32]{0,1:T(8,128)(2,1)S(1)} %copy-done.33), channel_id=1, source_target_pairs={{0,16},{16,0},{1,17},{17,1},{2,18},{18,2},{3,19},{19,3},{4,20},{20... | collective-permute-start | bytes 196616 | tf_op jit(solution)/shard_map/ppermute | solution.py:966
  42.9 6.3 collective-permute-start.6
  89.9 10.3 %collective-permute-start.10 = (bf16[128,1024]{1,0:T(8,128)(2,1)}, bf16[128,1024]{1,0:T(8,128)(2,1)S(1)}, u32[]{:S(2)}, u32[]{:S(2)}) collective-permute-start(bf16[128,1024]{1,0:T(8,128)(2,1)} %bitcast.220), channel_id=1, source_target_pairs={{0,12},{4,8},{8,4},{12,0},{1,13},{5,9},{9,5},{13,1},{2,14},{6,10},... | collective-permute-start | bytes 786440 | tf_op jit(solution)/shard_map/ppermute | solution.py:966
  91.5 13.9 %collective-permute-start.8 = (bf16[128,1024]{1,0:T(8,128)(2,1)}, bf16[128,1024]{1,0:T(8,128)(2,1)S(1)}, u32[]{:S(2)}, u32[]{:S(2)}) collective-permute-start(bf16[128,1024]{1,0:T(8,128)(2,1)} %bitcast.219), channel_id=1, source_target_pairs={{0,4},{4,0},{8,12},{12,8},{1,5},{5,1},{9,13},{13,9},{2,6},{6,2},{1... | collective-permute-start | bytes 786440 | tf_op jit(solution)/shard_map/ppermute | solution.py:966
  93.0 12.4 %collective-permute-start.9 = (bf16[128,1024]{1,0:T(8,128)(2,1)}, bf16[128,1024]{1,0:T(8,128)(2,1)S(1)}, u32[]{:S(2)}, u32[]{:S(2)}) collective-permute-start(bf16[128,1024]{1,0:T(8,128)(2,1)} %bitcast.218), channel_id=1, source_target_pairs={{0,8},{4,12},{8,0},{12,4},{1,9},{5,13},{9,1},{13,5},{2,10},{6,14},... | collective-permute-start | bytes 786440 | tf_op jit(solution)/shard_map/ppermute | solution.py:966
  117.3 3.6 collective-permute-start.13
  117.3 26.2 %collective-permute-start.14 = (bf16[128,1024]{1,0:T(8,128)(2,1)}, bf16[128,1024]{1,0:T(8,128)(2,1)S(1)}, u32[]{:S(2)}, u32[]{:S(2)}) collective-permute-start(bf16[128,1024]{1,0:T(8,128)(2,1)} %get-tuple-element.157), channel_id=1, source_target_pairs={{0,4},{4,0},{8,12},{12,8},{1,5},{5,1},{9,13},{13,9},{2,6},{6,2},{1... | collective-permute-start | bytes 786440 | tf_op jit(solution)/shard_map/ppermute | solution.py:966
  118.4 25.1 %collective-permute-start.15 = (bf16[128,1024]{1,0:T(8,128)(2,1)}, bf16[128,1024]{1,0:T(8,128)(2,1)S(1)}, u32[]{:S(2)}, u32[]{:S(2)}) collective-permute-start(bf16[128,1024]{1,0:T(8,128)(2,1)} %get-tuple-element.158), channel_id=1, source_target_pairs={{0,8},{4,12},{8,0},{12,4},{1,9},{5,13},{9,1},{13,5},{2,10},{6,14},... | collective-permute-start | bytes 786440 | tf_op jit(solution)/shard_map/ppermute | solution.py:966
  119.4 25.4 %collective-permute-start.16 = (bf16[128,1024]{1,0:T(8,128)(2,1)}, bf16[128,1024]{1,0:T(8,128)(2,1)S(1)}, u32[]{:S(2)}, u32[]{:S(2)}) collective-permute-start(bf16[128,1024]{1,0:T(8,128)(2,1)} %get-tuple-element.159), channel_id=1, source_target_pairs={{0,12},{4,8},{8,4},{12,0},{1,13},{5,9},{9,5},{13,1},{2,14},{6,10},... | collective-permute-start | bytes 786440 | tf_op jit(solution)/shard_map/ppermute | solution.py:966
  145.5 3.8 collective-permute-start.17
  163.7 13.0 %collective-permute-start.18 = (bf16[128,1024]{1,0:T(8,128)(2,1)}, bf16[128,1024]{1,0:T(8,128)(2,1)S(1)}, u32[]{:S(2)}, u32[]{:S(2)}) collective-permute-start(bf16[128,1024]{1,0:T(8,128)(2,1)} %get-tuple-element.164), channel_id=1, source_target_pairs={{0,4},{4,0},{8,12},{12,8},{1,5},{5,1},{9,13},{13,9},{2,6},{6,2},{1... | collective-permute-start | bytes 786440 | tf_op jit(solution)/shard_map/ppermute | solution.py:966
  163.8 12.9 %collective-permute-start.19 = (bf16[128,1024]{1,0:T(8,128)(2,1)}, bf16[128,1024]{1,0:T(8,128)(2,1)S(1)}, u32[]{:S(2)}, u32[]{:S(2)}) collective-permute-start(bf16[128,1024]{1,0:T(8,128)(2,1)} %get-tuple-element.165), channel_id=1, source_target_pairs={{0,8},{4,12},{8,0},{12,4},{1,9},{5,13},{9,1},{13,5},{2,10},{6,14},... | collective-permute-start | bytes 786440 | tf_op jit(solution)/shard_map/ppermute | solution.py:966
  164.8 14.1 %collective-permute-start.20 = (bf16[128,1024]{1,0:T(8,128)(2,1)}, bf16[128,1024]{1,0:T(8,128)(2,1)S(1)}, u32[]{:S(2)}, u32[]{:S(2)}) collective-permute-start(bf16[128,1024]{1,0:T(8,128)(2,1)} %get-tuple-element.166), channel_id=1, source_target_pairs={{0,12},{4,8},{8,4},{12,0},{1,13},{5,9},{9,5},{13,1},{2,14},{6,10},... | collective-permute-start | bytes 786440 | tf_op jit(solution)/shard_map/ppermute | solution.py:966
  179.5 23.8 %collective-permute-start.21 = (bf16[128,2048]{1,0:T(8,128)(2,1)S(1)}, bf16[128,2048]{1,0:T(8,128)(2,1)S(1)}, u32[]{:S(2)}, u32[]{:S(2)}) collective-permute-start(bf16[128,2048]{1,0:T(8,128)(2,1)S(1)} %copy-done.21), channel_id=1, source_target_pairs={{0,4},{4,0},{8,12},{12,8},{1,5},{5,1},{9,13},{13,9},{2,6},{6,2},{1... | collective-permute-start | bytes 1572872 | tf_op jit(solution)/shard_map/ppermute | solution.py:966
  181.1 24.6 %collective-permute-start.22 = (bf16[128,2048]{1,0:T(8,128)(2,1)S(1)}, bf16[128,2048]{1,0:T(8,128)(2,1)}, u32[]{:S(2)}, u32[]{:S(2)}) collective-permute-start(bf16[128,2048]{1,0:T(8,128)(2,1)S(1)} %copy-done.21), channel_id=1, source_target_pairs={{0,8},{4,12},{8,0},{12,4},{1,9},{5,13},{9,1},{13,5},{2,10},{6,14},... | collective-permute-start | bytes 1572872 | tf_op jit(solution)/shard_map/ppermute | solution.py:966
  182.0 23.7 %collective-permute-start.23 = (bf16[128,2048]{1,0:T(8,128)(2,1)S(1)}, bf16[128,2048]{1,0:T(8,128)(2,1)}, u32[]{:S(2)}, u32[]{:S(2)}) collective-permute-start(bf16[128,2048]{1,0:T(8,128)(2,1)S(1)} %copy-done.21), channel_id=1, source_target_pairs={{0,12},{4,8},{8,4},{12,0},{1,13},{5,9},{9,5},{13,1},{2,14},{6,10},... | collective-permute-start | bytes 1572872 | tf_op jit(solution)/shard_map/ppermute | solution.py:966
  183.0 37.8 %collective-permute-start.24 = (bf16[512,2048]{1,0:T(8,128)(2,1)S(1)}, bf16[512,2048]{1,0:T(8,128)(2,1)}, u32[]{:S(2)}, u32[]{:S(2)}) collective-permute-start(bf16[512,2048]{1,0:T(8,128)(2,1)S(1)} %copy-done.2), channel_id=1, source_target_pairs={{0,16},{16,0},{1,17},{17,1},{2,18},{18,2},{3,19},{19,3},{4,20},{20... | collective-permute-start | bytes 6291464 | tf_op jit(solution)/shard_map/ppermute | solution.py:966
  208.3 6.4 collective-permute-start.25
  233.6 98.4 %all-to-all-start = ((bf16[4,512,2048]{2,1,0:T(8,128)(2,1)}), bf16[4,512,2048]{2,1,0:T(8,128)(2,1)}, u32[]{:S(2)}, u32[]{:S(2)}) async-start(bf16[4,512,2048]{2,1,0:T(8,128)(2,1)} %broadcast_in_dim.8), calls=%async_computation.1 | async-start | bytes 16777216 | tf_op jit(solution)/shard_map/all_to_all | solution.py:1135
  239.3 200.5 %reduce-scatter.2.cloned.1.call-start = ((), (), s32[]{:S(2)}) async-start(), calls=%async_computation.7 | async-start | bytes 7864320 | tf_op jit(solution)/shard_map/reduce_scatter | solution.py:1134
  250.3 16.1 %collective-permute-start.26 = (bf16[512,2048]{1,0:T(8,128)(2,1)S(1)}, bf16[512,2048]{1,0:T(8,128)(2,1)S(1)}, u32[]{:S(2)}, u32[]{:S(2)}) collective-permute-start(bf16[512,2048]{1,0:T(8,128)(2,1)S(1)} %slice_bitcast_fusion), channel_id=1, source_target_pairs={{0,16},{16,0},{1,17},{17,1},{2,18},{18,2},{3,19},{19,3},{4,20},{20... | collective-permute-start | bytes 6291464 | tf_op jit(solution)/shard_map/ppermute | solution.py:966
  332.0 79.8 %collective-permute-start.34 = (bf16[2048,2048]{1,0:T(8,128)(2,1)}, bf16[2048,2048]{1,0:T(8,128)(2,1)}, u32[]{:S(2)}, u32[]{:S(2)}) collective-permute-start(bf16[2048,2048]{1,0:T(8,128)(2,1)} %bitcast.27.normed_ref), channel_id=1, source_target_pairs={{0,16},{16,0},{1,17},{17,1},{2,18},{18,2},{3,19},{19,3},{4,20},{20... | collective-permute-start | bytes 25165832 | tf_op jit(solution)/shard_map/ppermute | solution.py:966
  337.5 33.2 %collective-permute-start.27 = (bf16[128,2048]{1,0:T(8,128)(2,1)}, bf16[128,2048]{1,0:T(8,128)(2,1)}, u32[]{:S(2)}, u32[]{:S(2)}) collective-permute-start(bf16[128,2048]{1,0:T(8,128)(2,1)} %get-tuple-element.259), channel_id=1, source_target_pairs={{0,4},{4,0},{8,12},{12,8},{1,5},{5,1},{9,13},{13,9},{2,6},{6,2},{1... | collective-permute-start | bytes 1572872 | tf_op jit(solution)/shard_map/ppermute | solution.py:966
  338.9 33.7 %collective-permute-start.28 = (bf16[128,2048]{1,0:T(8,128)(2,1)}, bf16[128,2048]{1,0:T(8,128)(2,1)}, u32[]{:S(2)}, u32[]{:S(2)}) collective-permute-start(bf16[128,2048]{1,0:T(8,128)(2,1)} %get-tuple-element.261), channel_id=1, source_target_pairs={{0,8},{4,12},{8,0},{12,4},{1,9},{5,13},{9,1},{13,5},{2,10},{6,14},... | collective-permute-start | bytes 1572872 | tf_op jit(solution)/shard_map/ppermute | solution.py:966
  339.5 35.5 %collective-permute-start.29 = (bf16[128,2048]{1,0:T(8,128)(2,1)S(1)}, bf16[128,2048]{1,0:T(8,128)(2,1)}, u32[]{:S(2)}, u32[]{:S(2)}) collective-permute-start(bf16[128,2048]{1,0:T(8,128)(2,1)S(1)} %get-tuple-element.260), channel_id=1, source_target_pairs={{0,12},{4,8},{8,4},{12,0},{1,13},{5,9},{9,5},{13,1},{2,14},{6,10},... | collective-permute-start | bytes 1572872 | tf_op jit(solution)/shard_map/ppermute | solution.py:966
  342.2 36.0 %collective-permute-start.30 = (bf16[128,2048]{1,0:T(8,128)(2,1)}, bf16[128,2048]{1,0:T(8,128)(2,1)S(1)}, u32[]{:S(2)}, u32[]{:S(2)}) collective-permute-start(bf16[128,2048]{1,0:T(8,128)(2,1)} %get-tuple-element.257), channel_id=1, source_target_pairs={{0,1},{1,0},{2,3},{3,2},{4,5},{5,4},{6,7},{7,6},{8,9},{9,8},{10,11... | collective-permute-start | bytes 1572872 | tf_op jit(solution)/shard_map/ppermute | solution.py:966
  370.7 38.3 %collective-permute-start.31 = (bf16[128,2048]{1,0:T(8,128)(2,1)}, bf16[128,2048]{1,0:T(8,128)(2,1)S(1)}, u32[]{:S(2)}, u32[]{:S(2)}) collective-permute-start(bf16[128,2048]{1,0:T(8,128)(2,1)} %get-tuple-element.256), channel_id=1, source_target_pairs={{0,2},{1,3},{2,0},{3,1},{4,6},{5,7},{6,4},{7,5},{8,10},{9,11},{10,... | collective-permute-start | bytes 1572872 | tf_op jit(solution)/shard_map/ppermute | solution.py:966
  372.6 36.4 %collective-permute-start.32 = (bf16[128,2048]{1,0:T(8,128)(2,1)}, bf16[128,2048]{1,0:T(8,128)(2,1)}, u32[]{:S(2)}, u32[]{:S(2)}) collective-permute-start(bf16[128,2048]{1,0:T(8,128)(2,1)} %get-tuple-element.255), channel_id=1, source_target_pairs={{0,3},{1,2},{2,1},{3,0},{4,7},{5,6},{6,5},{7,4},{8,11},{9,10},{10,... | collective-permute-start | bytes 1572872 | tf_op jit(solution)/shard_map/ppermute | solution.py:966
  409.2 1.5 collective-permute-start.33
  439.8 33.3 %all-to-all-start.1 = ((bf16[8,64,1536]{2,1,0:T(8,128)(2,1)}), bf16[8,64,1536]{2,1,0:T(8,128)(2,1)S(1)}, u32[]{:S(2)}, u32[]{:S(2)}) async-start(bf16[8,64,1536]{2,1,0:T(8,128)(2,1)} %bitcast.186), calls=%async_computation.2 | async-start | bytes 3145728 | tf_op jit(solution)/shard_map/all_to_all | solution.py:1182
  443.5 79.8 %all-gather.11.cloned.1.call-start = ((), (), s32[]{:S(2)}) async-start(), calls=%async_computation.8 | async-start | bytes 3276800 | tf_op jit(solution)/shard_map/all_gather | solution.py:1240
  444.1 181.4 %all-gather.13.cloned.1.call-start = ((), (), s32[]{:S(2)}) async-start(), calls=%async_computation.9 | async-start | bytes 7864320 | tf_op jit(solution)/shard_map/all_gather | solution.py:1250
  453.3 21.1 %collective-permute-start.35 = (f32[128,2048]{1,0:T(8,128)}, f32[128,2048]{1,0:T(8,128)}, u32[]{:S(2)}, u32[]{:S(2)}) collective-permute-start(f32[128,2048]{1,0:T(8,128)} %slice.168), channel_id=1, source_target_pairs={{0,16},{16,0},{1,17},{17,1},{2,18},{18,2},{3,19},{19,3},{4,20},{20... | collective-permute-start | bytes 3145736 | tf_op jit(solution)/shard_map/ppermute | solution.py:966
  478.9 44.4 %all-to-all-start.2 = ((bf16[8,256,704]{1,2,0:T(8,128)(2,1)}), bf16[8,256,704]{1,2,0:T(8,128)(2,1)S(1)}, u32[]{:S(2)}, u32[]{:S(2)}) async-start(bf16[8,256,704]{1,2,0:T(8,128)(2,1)} %bitcast.170), calls=%async_computation.3 | async-start | bytes 5767168 | tf_op jit(solution)/shard_map/all_to_all | solution.py:1182
  528.0 53.7 %all-to-all-start.3 = ((bf16[8,256,704]{1,2,0:T(8,128)(2,1)}), bf16[8,256,704]{1,2,0:T(8,128)(2,1)S(1)}, u32[]{:S(2)}, u32[]{:S(2)}) async-start(bf16[8,256,704]{1,2,0:T(8,128)(2,1)} %bitcast.169), calls=%async_computation.4 | async-start | bytes 5767168 | tf_op jit(solution)/shard_map/all_to_all | solution.py:1182
  533.8 36.0 %collective-permute-start.36 = (f32[15,2048]{1,0:T(8,128)S(1)}, f32[15,2048]{1,0:T(8,128)S(1)}, u32[]{:S(2)}, u32[]{:S(2)}) collective-permute-start(f32[15,2048]{1,0:T(8,128)S(1)} %fusion.17), channel_id=1, source_target_pairs={{0,4},{4,0},{8,12},{12,8},{1,5},{5,1},{9,13},{13,9},{2,6},{6,2},{1... | collective-permute-start | bytes 368648 | tf_op jit(solution)/shard_map/ppermute | solution.py:966
  535.9 34.0 %collective-permute-start.37 = (f32[15,2048]{1,0:T(8,128)S(1)}, f32[15,2048]{1,0:T(8,128)S(1)}, u32[]{:S(2)}, u32[]{:S(2)}) collective-permute-start(f32[15,2048]{1,0:T(8,128)S(1)} %fusion.17), channel_id=1, source_target_pairs={{0,8},{4,12},{8,0},{12,4},{1,9},{5,13},{9,1},{13,5},{2,10},{6,14},... | collective-permute-start | bytes 368648 | tf_op jit(solution)/shard_map/ppermute | solution.py:966
  537.4 35.7 %collective-permute-start.38 = (f32[15,2048]{1,0:T(8,128)S(1)}, f32[15,2048]{1,0:T(8,128)S(1)}, u32[]{:S(2)}, u32[]{:S(2)}) collective-permute-start(f32[15,2048]{1,0:T(8,128)S(1)} %fusion.17), channel_id=1, source_target_pairs={{0,12},{4,8},{8,4},{12,0},{1,13},{5,9},{9,5},{13,1},{2,14},{6,10},... | collective-permute-start | bytes 368648 | tf_op jit(solution)/shard_map/ppermute | solution.py:966
  (50 other events, 610.0 us)
Sparse Core Ops, SparseCore 0:
  41.9 126.4 all-gather.6
  170.5 44.1 all-gather.8
  242.5 114.4 reduce-scatter.1
  445.6 64.2 all-gather.10
  511.3 114.1 all-gather.12
